TPU v7x, 256 devices: a whole 4x4x8 slice. The times are simulated.
256 devices in a mesh: depth: 2 (over z_lo), row: 8 (over x, core), col: 16 (over z_hi, y).
Axes of the slice: x: 4, y: 4, z: 8 (z_hi: 4, z_lo: 2; z = z_hi * 2 + z_lo), core: 2. Of those that a mesh axis runs over, the one named last changes fastest.
Arguments:
- normed: bfloat16 [4096, 6144], P(('depth', 'col'), 'row'), may hold values from -6 to 6
- positions: int32 [4096], P(('depth', 'col')), may hold values from 0 to 1567, as said below
- cotangent: bfloat16 [4096, 6144], P(('depth', 'col'), 'row'), may hold values from -4 to 4
- w_in: bfloat16 [6144, 12288], P('row', 'col'), may hold values from -0.078125 to 0.078125
- b_in: float32 [12288], P('col'), may hold values from -4 to 4
- w_out: bfloat16 [12288, 6144], P('col', 'row'), may hold values from -0.0546875 to 0.0546875
Outputs:
- d_normed: bfloat16 [4096, 6144], P(('depth', 'col'), 'row')
- d_w_in: float32 [6144, 12288], P('row', 'col')
- d_b_in: float32 [12288], P('col')
- d_w_out: float32 [12288, 6144], P('col', 'row')
Inputs may be any that keep to these rules, and one draw needn't show every extreme that they name: positions holds 16 clips of 256 consecutive tokens; in each clip the same 256 // 8 of the 196 spatial places (ascending, always including places 0 and 195) are kept in each of the 8 frames, position = frame * 196 + place, frames ascending.
All inputs are finite; a program needn't handle non-finite values.
Results may differ from a plain program's by a relative error of at most 0.03.
Values may be sent and summed in bfloat16 or wider, within the bound.
No kernel may reach another device: no remote copies, remote signals or barrier semaphores. Data moves between devices by JAX's collectives and lax.ppermute only.
A program may use at most 128 MiB of HBM per device.

v0:
```python
import jax
import jax.numpy as jnp
from jax import lax
from jax.experimental import pallas as pl
from jax.sharding import PartitionSpec as P

D = 6144
AXES = ("depth", "row", "col")

coeff = 0.7978845608028654


def sincos(positions, first, width):
    places = positions.astype(jnp.float32)[:, None]
    column = first + jnp.arange(width, dtype=jnp.int32)
    expo = (2 * (column // 2)).astype(jnp.float32) / jnp.float32(D)
    freq = jnp.power(jnp.float32(10000.0), -expo)
    angle = places * freq[None, :]
    return jnp.where((column % 2 == 0)[None, :], jnp.sin(angle), jnp.cos(angle))


def gelu_pair(value):
    inner = coeff * (value + 0.044715 * value * value * value)
    slope = jnp.tanh(inner)
    out = 0.5 * value * (1.0 + slope)
    grad = 0.5 * (1.0 + slope) + 0.5 * value * (1.0 - slope * slope) * coeff * (
        1.0 + 3.0 * 0.044715 * value * value
    )
    return (out, grad)


def moves(shift):
    def index(d, x, c, z, y):
        return ((d % 2) * 8 + (x % 4) * 2 + c % 2) * 16 + (z % 4) * 4 + y % 4

    return [
        (index(d, x, c, z, y), index(*shift(d, x, c, z, y)))
        for d in range(2)
        for x in range(4)
        for c in range(2)
        for z in range(4)
        for y in range(4)
    ]


CORE = moves(lambda d, x, c, z, y: (d, x, c + 1, z, y))
DEPTH = moves(lambda d, x, c, z, y: (d + 1, x, c, z, y))
Y_BY = [moves(lambda d, x, c, z, y, k=k: (d, x, c, z, y + k)) for k in range(4)]
Z_BY = [moves(lambda d, x, c, z, y, j=j: (d, x, c, z + j, y)) for j in range(4)]
X_SETS = [[c + 2 * x for x in range(4)] for c in range(2)]

Y_SETS = [[z * 4 + y for y in range(4)] for z in range(4)]


def send(value, pairs):
    return lax.ppermute(value, AXES, pairs)


def dot(a, b, contract, kind=jnp.float32):
    return lax.dot_general(
        a, b, ((contract[:1], contract[1:]), ((), ())), preferred_element_type=jnp.float32
    ).astype(kind)


def share_kernel(d_ref, w_ref, *outs):
    for k, out in zip((2, 1, 3, 0), outs):
        rows = d_ref[:, k].reshape(out.shape[0], d_ref.shape[3])
        out[...] = lax.dot_general(
            rows, w_ref[...], (((1,), (1,)), ((), ())), preferred_element_type=jnp.float32
        ).astype(out.dtype)


def all_shares(d_pre, w):
    rows, wide, hidden = 4 * d_pre.shape[2], w.shape[0], w.shape[1]
    tile = 256
    return pl.pallas_call(
        share_kernel,
        grid=(wide // tile,),
        in_specs=[
            pl.BlockSpec(d_pre.shape, lambda n: (0, 0, 0, 0)),
            pl.BlockSpec((tile, hidden), lambda n: (n, 0)),
        ],
        out_specs=[pl.BlockSpec((rows, tile), lambda n: (0, n))] * 4,
        out_shape=[jax.ShapeDtypeStruct((rows, wide), kind) for kind in [d_pre.dtype] * 3 + [jnp.float32]],
        cost_estimate=pl.CostEstimate(
            flops=8 * rows * wide * hidden, bytes_accessed=2 * (d_pre.size + w.size + 5 * rows * wide), transcendentals=0
        ),
    )(d_pre, w)


def columns_kernel(a_ref, b_ref, *refs):
    product = lax.dot_general(
        a_ref[...], b_ref[...], (((0,), (0,)), ((), ())), preferred_element_type=jnp.float32
    )
    for got_ref in refs[:-1]:
        product = product + got_ref[...].astype(jnp.float32)
    refs[-1][...] = product.astype(refs[-1].dtype)


def columns_by(a, b, *got):
    tile = 128
    rows, size = a.shape[1], b.shape[1]
    return pl.pallas_call(
        columns_kernel,
        grid=(rows // tile,),
        in_specs=[
            pl.BlockSpec((a.shape[0], tile), lambda n: (0, n)),
            pl.BlockSpec(b.shape, lambda n: (0, 0)),
            *[pl.BlockSpec((tile, size), lambda n: (n, 0))] * len(got),
        ],
        out_specs=pl.BlockSpec((tile, size), lambda n: (n, 0)),
        out_shape=jax.ShapeDtypeStruct((rows, size), a.dtype),
        cost_estimate=pl.CostEstimate(
            flops=2 * a.size * size, bytes_accessed=2 * (a.size + b.size + 2 * rows * size), transcendentals=0
        ),
    )(a, b, *got)


def on_device(normed, positions, cotangent, w_in, b_in, w_out):
    bf, f32 = jnp.bfloat16, jnp.float32
    width = w_in.shape[0]
    hidden = w_in.shape[1]
    row = lax.axis_index("row")
    core = row % 2
    half = normed.shape[0] // 2

    def after(value, *others):
        return lax.optimization_barrier((value, *others))[0]

    def swap_x(value):
        return lax.all_to_all(value, "row", 0, 0, tiled=True, axis_index_groups=X_SETS)

    def scatter_x(part):
        return jnp.sum(swap_x(part).astype(f32), axis=0)

    def gather_x(own):
        return swap_x(jnp.broadcast_to(own[None], (4,) + own.shape))

    inputs = (normed.astype(f32) + sincos(positions, row * width, width)).astype(bf)
    both = jnp.stack([inputs, cotangent])
    mine = lax.dynamic_slice_in_dim(both, core * half, half, 1)
    other = send(lax.dynamic_slice_in_dim(both, (1 - core) * half, half, 1), CORE)
    x_half = jnp.concatenate([mine[0], other[0]], axis=1)
    c_half = jnp.concatenate([mine[1], other[1]], axis=1)
    w_in_got = send(w_in, CORE)
    w_out_got = send(w_out, CORE)
    w_in_all = jnp.concatenate([w_in, w_in_got], axis=0)
    w_out_all = jnp.concatenate([w_out, w_out_got], axis=1)

    x_one, x_three, x_two = (send(x_half, Z_BY[4 - j]) for j in (1, 3, 2))
    c_four = jnp.broadcast_to(after(c_half, x_half)[None], (4,) + c_half.shape)
    c_four = lax.all_to_all(c_four, "col", 0, 0, tiled=True, axis_index_groups=Y_SETS)
    y = lax.axis_index("col") % 4
    c_own = lax.dynamic_slice_in_dim(jnp.concatenate([c_four, c_four]), y, 4, 0)
    x_own = jnp.concatenate([x_half, x_one, x_two, x_three])

    x_up, x_down = send(x_own, Y_BY[3]), send(x_own, Y_BY[1])
    c_own = after(c_own, x_own, w_in_got, w_out_got)
    c_up, c_down = send(c_own, Z_BY[3]), send(c_own, Z_BY[1])
    parts = [dot(x_own, w_in_all, (1, 0), bf), None, None, None]
    x_up, x_down = after((x_up, x_down), parts[0])
    rows = 2 * half
    far = [send(x_up[:rows], Y_BY[3]), send(x_down[rows:], Y_BY[1])]
    parts[1], parts[3] = dot(x_up, w_in_all, (1, 0), bf), dot(x_down, w_in_all, (1, 0), bf)
    x_far = jnp.concatenate(after(far, parts[1], parts[3]))
    parts[2] = dot(x_far, w_in_all, (1, 0), bf)
    xs = [x_own, x_up, x_far, x_down]
    parts = [part.reshape(4, half, hidden) for part in parts]

    c_up, c_down = after((c_up, c_down), parts)
    c_far = jnp.concatenate([send(c_up[:2], Z_BY[3]), send(c_down[2:], Z_BY[1])])
    cs = [c.reshape(-1, 2 * width) for c in (c_own, c_up, c_far, c_down)]

    near = scatter_x(jnp.stack([parts[k] for k in (0, 1, 3)], axis=1))
    last = scatter_x(after(parts[2], near)[:, None])
    pre = jnp.concatenate([near[:2], last, near[2:]]) + b_in[None, None, :]
    act, slope = gelu_pair(pre)
    act_all = gather_x(act.astype(bf))

    d_parts = jnp.stack([dot(c, w_out_all, (1, 1), bf).reshape(4, half, hidden) for c in cs])
    d_parts, cs = after((d_parts, cs), act_all)
    d_act = swap_x(d_parts)
    c_mine = jnp.concatenate([c[:, :width] for c in cs])
    c_other = jnp.concatenate([c[:, width:] for c in cs])

    act_all = act_all.reshape(-1, hidden)
    cut = hidden // 2
    act_cuts = [act_all[:, :cut], act_all[:, cut:]]
    out_got = [send(dot(a, c_other, (0, 0), bf), CORE) for a in act_cuts]
    out_mine = [(dot(a, c_mine, (0, 0)) + got.astype(f32)).astype(bf) for a, got in zip(act_cuts, out_got)]
    out_deep = [send(mine, DEPTH) for mine in out_mine]

    d_act = jnp.sum(d_act.astype(f32), axis=0)
    d_pre_all = gather_x((d_act * slope).astype(bf))

    cut = width // 2
    x_mine = [jnp.concatenate([x[:, i * cut : (i + 1) * cut] for x in xs]) for i in (0, 1)]
    x_other = [jnp.concatenate([x[:, i * cut : (i + 1) * cut] for x in xs]) for i in (2, 3)]
    x_other[1] = jnp.concatenate([x_other[1], jnp.ones((x_other[1].shape[0], 16), bf)], axis=1)
    d_raw = after(d_pre_all, x_mine, x_other)
    d_pre_all = d_raw.swapaxes(0, 1)
    d_pre_rows = d_pre_all.reshape(-1, hidden)
    d_pre_rows = after(d_pre_rows, out_mine)
    in_other = [columns_by(x_other[0], d_pre_rows), dot(x_other[1], d_pre_rows, (0, 0), bf)]
    in_got = [send(other, CORE) for other in in_other]
    *shares, total = all_shares(after(d_raw, in_other), w_in_all)
    got = [send(share, Y_BY[k]) for share, k in zip(shares, (2, 1, 3))]
    in_got = after(in_got, *shares)
    out_deep = after(out_deep, *shares)
    d_w_out = jnp.concatenate([mine.astype(f32) + deep.astype(f32) for mine, deep in zip(out_mine, out_deep)])
    in_mine = [columns_by(x, d_pre_rows, got) for x, got in zip(x_mine, in_got)]
    bias = (in_other[1][cut:].astype(f32) + in_got[1][cut:].astype(f32)).astype(bf)
    in_both = [in_mine[0], jnp.concatenate([in_mine[1], bias])]
    in_deep = [send(mine, DEPTH) for mine in in_both]
    d_w_in = jnp.concatenate([mine.astype(f32) + deep[:cut].astype(f32) for mine, deep in zip(in_mine, in_deep)])

    for term in after(got, in_both):
        total = total + term.astype(f32)
    total = total.reshape(4, half, 2 * width)
    d_half = total[0]
    for term in after([send(total[j].astype(bf), Z_BY[j]) for j in range(1, 4)], in_deep):
        d_half = d_half + term.astype(f32)
    d_half = d_half.astype(bf)
    mine, got = d_half[:, :width], send(d_half[:, width:], CORE)
    first = jnp.where(core == 0, mine, got)
    second = jnp.where(core == 0, got, mine)
    d_normed = jnp.concatenate([first, second], axis=0)
    d_b_in = after(bias[0], d_normed, d_w_in, d_w_out).astype(f32) + in_deep[1][cut].astype(f32)
    return (d_normed, d_w_in, d_b_in, d_w_out)


def solution(mesh):
    placed = (
        P(("depth", "col"), "row"),
        P(("depth", "col")),
        P(("depth", "col"), "row"),
        P("row", "col"),
        P("col"),
        P("col", "row"),
    )
    return jax.shard_map(
        on_device,
        mesh=mesh,
        in_specs=placed,
        out_specs=(P(("depth", "col"), "row"), P("row", "col"), P("col"), P("col", "row")),
        check_vma=False,
    )
```

profile of v0, /device:TPU:1, one launch (start us, length us, event | category | flops | bytes accessed | tf_op | source)
XLA Modules:
  0.0 247.0 jit_solution(13320703846853265444)
XLA Ops:
  11.3 5.1 %collective-permute-start.2 = (bf16[64,1536]{1,0:T(8,128)(2,1)S(1)}, bf16[64,1536]{1,0:T(8,128)(2,1)S(1)}, u32[]{:S(2)}, u32[]{:S(2)}) collective-permute-start(bf16[64,1536]{1,0:T(8,128)(2,1)S(1)} %pad_maximum_fusion.17), channel_id=1, source_target_pairs={{0,8},{1,9},{2,10},{3,11},{4,12},{5,13},{6,14},{7,15},{8,0},{9,1},... | collective-permute-start | bytes 589832 | tf_op jit(solution)/shard_map/ppermute | solution.py:56
  19.8 4.2 %all-to-all-start = ((bf16[4,64,1536]{2,1,0:T(8,128)(2,1)}), bf16[4,64,1536]{2,1,0:T(8,128)(2,1)S(1)}, u32[]{:S(2)}, u32[]{:S(2)}) async-start(bf16[4,64,1536]{2,1,0:T(8,128)(2,1)} %broadcast_in_dim.17), calls=%async_computation | async-start | bytes 1572864 | tf_op jit(solution)/shard_map/all_to_all | solution.py:152
  25.0 3.5 %collective-permute-done.2 = bf16[64,1536]{1,0:T(8,128)(2,1)S(1)} collective-permute-done((bf16[64,1536]{1,0:T(8,128)(2,1)S(1)}, bf16[64,1536]{1,0:T(8,128)(2,1)S(1)}, u32[]{:S(2)}, u32[]{:S(2)}) %collective-permute-start.2) | collective-permute-done | bytes 196640 | tf_op jit(solution)/shard_map/ppermute | solution.py:56
  28.6 6.5 %collective-permute-done.1 = bf16[64,1536]{1,0:T(8,128)(2,1)S(1)} collective-permute-done((bf16[64,1536]{1,0:T(8,128)(2,1)S(1)}, bf16[64,1536]{1,0:T(8,128)(2,1)S(1)}, u32[]{:S(2)}, u32[]{:S(2)}) %collective-permute-start.1) | collective-permute-done | bytes 196640 | tf_op jit(solution)/shard_map/ppermute | solution.py:56
  47.5 6.8 %collective-permute-done.8 = bf16[256,1536]{1,0:T(8,128)(2,1)S(1)} collective-permute-done((bf16[256,1536]{1,0:T(8,128)(2,1)S(1)}, bf16[256,1536]{1,0:T(8,128)(2,1)S(1)}, u32[]{:S(2)}, u32[]{:S(2)}) %collective-permute-start.8) | collective-permute-done | bytes 786464 | tf_op jit(solution)/shard_map/ppermute | solution.py:56
  64.7 4.0 %all-to-all-start.1 = ((bf16[4,3,64,768]{3,2,1,0:T(8,128)(2,1)}), bf16[4,3,64,768]{3,2,1,0:T(8,128)(2,1)S(1)}, u32[]{:S(2)}, u32[]{:S(2)}) async-start(bf16[4,3,64,768]{3,2,1,0:T(8,128)(2,1)} %pad_maximum_fusion.5), calls=%async_computation.1 | async-start | bytes 2359296 | tf_op jit(solution)/shard_map/all_to_all | solution.py:131
  71.1 3.4 %convolution_convert_fusion.10 = bf16[256,768]{1,0:T(8,128)(2,1)} fusion(bf16[256,1536]{1,0:T(8,128)(2,1)S(1)} %bitcast.56, bf16[768,1536]{1,0:T(8,128)(2,1)} %constant_dynamic-update-slice_fusion), kind=kOutput, calls=%fused_computation.25 | convolution fusion | flops 604176384 | bytes 3538944 | tf_op jit(solution)/shard_map/dot_general | solution.py:60
  78.8 3.9 %all-to-all-done.1 = bf16[4,3,64,768]{3,2,1,0:T(8,128)(2,1)S(1)} async-done(((bf16[4,3,64,768]{3,2,1,0:T(8,128)(2,1)}), bf16[4,3,64,768]{3,2,1,0:T(8,128)(2,1)S(1)}, u32[]{:S(2)}, u32[]{:S(2)}) %all-to-all-start.1) | async-done | bytes 1179680 | tf_op jit(solution)/shard_map/all_to_all | solution.py:131
  82.9 3.5 %all-to-all-start.2 = ((bf16[4,1,64,768]{3,2,1,0:T(8,128)(2,1)}), bf16[4,1,64,768]{3,2,1,0:T(8,128)(2,1)S(1)}, u32[]{:S(2)}, u32[]{:S(2)}) async-start(bf16[4,1,64,768]{3,2,1,0:T(8,128)(2,1)} %bitcast.21), calls=%async_computation.2 | async-start | bytes 786432 | tf_op jit(solution)/shard_map/all_to_all | solution.py:131
  98.9 4.2 %all-to-all-start.3 = ((bf16[4,4,64,768]{3,2,1,0:T(8,128)(2,1)}), bf16[4,4,64,768]{3,2,1,0:T(8,128)(2,1)S(1)}, u32[]{:S(2)}, u32[]{:S(2)}) async-start(bf16[4,4,64,768]{3,2,1,0:T(8,128)(2,1)} %broadcast_in_dim.19), calls=%async_computation.3 | async-start | bytes 3145728 | tf_op jit(solution)/shard_map/all_to_all | solution.py:131
  113.5 5.5 %all-to-all-done.3 = bf16[4,4,64,768]{3,2,1,0:T(8,128)(2,1)S(1)} async-done(((bf16[4,4,64,768]{3,2,1,0:T(8,128)(2,1)}), bf16[4,4,64,768]{3,2,1,0:T(8,128)(2,1)S(1)}, u32[]{:S(2)}, u32[]{:S(2)}) %all-to-all-start.3) | async-done | bytes 1572896 | tf_op jit(solution)/shard_map/all_to_all | solution.py:131
  120.2 3.6 %all-to-all-start.4 = ((bf16[4,4,64,768]{3,2,1,0:T(8,128)(2,1)}), bf16[4,4,64,768]{3,2,1,0:T(8,128)(2,1)S(1)}, u32[]{:S(2)}, u32[]{:S(2)}) async-start(bf16[4,4,64,768]{3,2,1,0:T(8,128)(2,1)} %pad_maximum_fusion.2), calls=%async_computation.4 | async-start | bytes 3145728 | tf_op jit(solution)/shard_map/all_to_all | solution.py:131
  133.4 5.8 %collective-permute-start.14 = (bf16[384,768]{1,0:T(8,128)(2,1)}, bf16[384,768]{1,0:T(8,128)(2,1)}, u32[]{:S(2)}, u32[]{:S(2)}) collective-permute-start(bf16[384,768]{1,0:T(8,128)(2,1)} %convolution_convert_fusion.2), channel_id=1, source_target_pairs={{0,16},{1,17},{2,18},{3,19},{4,20},{5,21},{6,22},{7,23},{8,24},{9,... | collective-permute-start | bytes 1769480 | tf_op jit(solution)/shard_map/ppermute | solution.py:56
  141.3 4.6 %all-to-all-start.5 = ((bf16[4,4,64,768]{3,2,1,0:T(8,128)(2,1)}), bf16[4,4,64,768]{3,2,1,0:T(8,128)(2,1)S(1)}, u32[]{:S(2)}, u32[]{:S(2)}) async-start(bf16[4,4,64,768]{3,2,1,0:T(8,128)(2,1)} %broadcast_in_dim.20), calls=%async_computation.5 | async-start | bytes 3145728 | tf_op jit(solution)/shard_map/all_to_all | solution.py:131
  148.1 5.3 %collective-permute-start.15 = (bf16[384,768]{1,0:T(8,128)(2,1)S(1)}, bf16[384,768]{1,0:T(8,128)(2,1)S(1)}, u32[]{:S(2)}, u32[]{:S(2)}) collective-permute-start(bf16[384,768]{1,0:T(8,128)(2,1)S(1)} %convolution_convert_fusion.1), channel_id=1, source_target_pairs={{0,16},{1,17},{2,18},{3,19},{4,20},{5,21},{6,22},{7,23},{8,24},{9,... | collective-permute-start | bytes 1769480 | tf_op jit(solution)/shard_map/ppermute | solution.py:56
  163.1 4.2 %shard_map.93 = bf16[384,768]{1,0:T(8,128)(2,1)} custom-call(bf16[1024,384]{1,0:T(8,128)(2,1)} %pad_maximum_fusion.10.a_ref, bf16[1024,768]{1,0:T(8,128)(2,1)} %bitcast.51), custom_call_target="tpu_custom_call" | custom-call | flops 603979776 | bytes 3538944 | tf_op jit(solution)/shard_map/pallas_call | solution.py:103
  167.3 6.1 %collective-permute-start.19 = (bf16[384,768]{1,0:T(8,128)(2,1)}, bf16[384,768]{1,0:T(8,128)(2,1)}, u32[]{:S(2)}, u32[]{:S(2)}) collective-permute-start(bf16[384,768]{1,0:T(8,128)(2,1)} %shard_map.93), channel_id=1, source_target_pairs={{0,16},{1,17},{2,18},{3,19},{4,20},{5,21},{6,22},{7,23},{8,24},{9,... | collective-permute-start | bytes 1769480 | tf_op jit(solution)/shard_map/ppermute | solution.py:56
  175.1 7.2 %shard_map.94 = (bf16[256,1536]{1,0:T(8,128)(2,1)}, bf16[256,1536]{1,0:T(8,128)(2,1)}, bf16[256,1536]{1,0:T(8,128)(2,1)}, f32[256,1536]{1,0:T(8,128)}) custom-call(bf16[4,4,64,768]{3,2,1,0:T(8,128)(2,1)} %copy-done.1, bf16[1536,768]{1,0:T(8,128)(2,1)} %constant_dynamic-update-slice_fusion.2.w_ref), custom_call_target="tpu_custom_call" | custom-call | flops 2415919104 | bytes 7864320 | tf_op jit(solution)/shard_map/pallas_call | solution.py:76
  193.4 4.3 %shard_map.95 = bf16[384,768]{1,0:T(8,128)(2,1)} custom-call(bf16[1024,384]{1,0:T(8,128)(2,1)} %pad_maximum_fusion.8.a_ref, bf16[1024,768]{1,0:T(8,128)(2,1)} %bitcast.52, bf16[384,768]{1,0:T(8,128)(2,1)} %collective-permute-done.19.refs_0_), custom_call_target="tpu_custom_call" | custom-call | flops 603979776 | bytes 3538944 | tf_op jit(solution)/shard_map/pallas_call | solution.py:103
  197.8 4.3 %shard_map.96 = bf16[384,768]{1,0:T(8,128)(2,1)} custom-call(bf16[1024,384]{1,0:T(8,128)(2,1)} %pad_maximum_fusion.9.a_ref, bf16[1024,768]{1,0:T(8,128)(2,1)} %bitcast.53, bf16[400,768]{1,0:T(8,128)(2,1)} %copy-done.30), custom_call_target="tpu_custom_call" | custom-call | flops 603979776 | bytes 3538944 | tf_op jit(solution)/shard_map/pallas_call | solution.py:103
  205.3 15.0 %collective-permute-done.17 = bf16[256,1536]{1,0:T(8,128)(2,1)S(1)} collective-permute-done((bf16[256,1536]{1,0:T(8,128)(2,1)}, bf16[256,1536]{1,0:T(8,128)(2,1)S(1)}, u32[]{:S(2)}, u32[]{:S(2)}) %collective-permute-start.17) | collective-permute-done | bytes 786464 | tf_op jit(solution)/shard_map/ppermute | solution.py:56
  222.1 4.0 %collective-permute-start.22 = (bf16[64,1536]{1,0:T(8,128)(2,1)S(1)}, bf16[64,1536]{1,0:T(8,128)(2,1)S(1)}, u32[]{:S(2)}, u32[]{:S(2)}) collective-permute-start(bf16[64,1536]{1,0:T(8,128)(2,1)S(1)} %get-tuple-element.71), channel_id=1, source_target_pairs={{0,8},{1,9},{2,10},{3,11},{4,12},{5,13},{6,14},{7,15},{8,0},{9,1},... | collective-permute-start | bytes 589832 | tf_op jit(solution)/shard_map/ppermute | solution.py:56
  229.1 5.3 %collective-permute-done.21 = bf16[64,1536]{1,0:T(8,128)(2,1)S(1)} collective-permute-done((bf16[64,1536]{1,0:T(8,128)(2,1)S(1)}, bf16[64,1536]{1,0:T(8,128)(2,1)S(1)}, u32[]{:S(2)}, u32[]{:S(2)}) %collective-permute-start.21) | collective-permute-done | bytes 196640 | tf_op jit(solution)/shard_map/ppermute | solution.py:56
  234.4 6.2 %collective-permute-done.22 = bf16[64,1536]{1,0:T(8,128)(2,1)S(1)} collective-permute-done((bf16[64,1536]{1,0:T(8,128)(2,1)S(1)}, bf16[64,1536]{1,0:T(8,128)(2,1)S(1)}, u32[]{:S(2)}, u32[]{:S(2)}) %collective-permute-start.22) | collective-permute-done | bytes 196640 | tf_op jit(solution)/shard_map/ppermute | solution.py:56
  (224 shorter events, 119.3 us)
Async XLA Ops:
  8.3 30.9 %collective-permute-start.4 = (bf16[768,768]{1,0:T(8,128)(2,1)}, bf16[768,768]{1,0:T(8,128)(2,1)}, u32[]{:S(2)}, u32[]{:S(2)}) collective-permute-start(bf16[768,768]{1,0:T(8,128)(2,1)} %param.9), channel_id=1, source_target_pairs={{0,16},{1,17},{2,18},{3,19},{4,20},{5,21},{6,22},{7,23},{8,24},{9,... | collective-permute-start | bytes 3538952 | tf_op jit(solution)/shard_map/ppermute | solution.py:56
  8.4 30.8 %collective-permute-start.5 = (bf16[768,768]{1,0:T(8,128)(2,1)}, bf16[768,768]{1,0:T(8,128)(2,1)}, u32[]{:S(2)}, u32[]{:S(2)}) collective-permute-start(bf16[768,768]{1,0:T(8,128)(2,1)} %param.11), channel_id=1, source_target_pairs={{0,16},{1,17},{2,18},{3,19},{4,20},{5,21},{6,22},{7,23},{8,24},{9,... | collective-permute-start | bytes 3538952 | tf_op jit(solution)/shard_map/ppermute | solution.py:56
  11.3 17.2 %collective-permute-start.2 = (bf16[64,1536]{1,0:T(8,128)(2,1)S(1)}, bf16[64,1536]{1,0:T(8,128)(2,1)S(1)}, u32[]{:S(2)}, u32[]{:S(2)}) collective-permute-start(bf16[64,1536]{1,0:T(8,128)(2,1)S(1)} %pad_maximum_fusion.17), channel_id=1, source_target_pairs={{0,8},{1,9},{2,10},{3,11},{4,12},{5,13},{6,14},{7,15},{8,0},{9,1},... | collective-permute-start | bytes 589832 | tf_op jit(solution)/shard_map/ppermute | solution.py:56
  16.4 18.6 %collective-permute-start.1 = (bf16[64,1536]{1,0:T(8,128)(2,1)S(1)}, bf16[64,1536]{1,0:T(8,128)(2,1)S(1)}, u32[]{:S(2)}, u32[]{:S(2)}) collective-permute-start(bf16[64,1536]{1,0:T(8,128)(2,1)S(1)} %pad_maximum_fusion.17), channel_id=1, source_target_pairs={{0,12},{1,13},{2,14},{3,15},{4,0},{5,1},{6,2},{7,3},{8,4},{9,5},{1... | collective-permute-start | bytes 589832 | tf_op jit(solution)/shard_map/ppermute | solution.py:56
  19.8 19.1 %all-to-all-start = ((bf16[4,64,1536]{2,1,0:T(8,128)(2,1)}), bf16[4,64,1536]{2,1,0:T(8,128)(2,1)S(1)}, u32[]{:S(2)}, u32[]{:S(2)}) async-start(bf16[4,64,1536]{2,1,0:T(8,128)(2,1)} %broadcast_in_dim.17), calls=%async_computation | async-start | bytes 1572864 | tf_op jit(solution)/shard_map/all_to_all | solution.py:152
  35.1 19.2 %collective-permute-start.8 = (bf16[256,1536]{1,0:T(8,128)(2,1)S(1)}, bf16[256,1536]{1,0:T(8,128)(2,1)S(1)}, u32[]{:S(2)}, u32[]{:S(2)}) collective-permute-start(bf16[256,1536]{1,0:T(8,128)(2,1)S(1)} %pad_maximum_fusion.6), channel_id=1, source_target_pairs={{0,3},{1,0},{2,1},{3,2},{4,7},{5,4},{6,5},{7,6},{8,11},{9,8},{10,9... | collective-permute-start | bytes 2359304 | tf_op jit(solution)/shard_map/ppermute | solution.py:56
  37.9 19.6 %collective-permute-start.9 = (bf16[256,1536]{1,0:T(8,128)(2,1)S(1)}, bf16[256,1536]{1,0:T(8,128)(2,1)}, u32[]{:S(2)}, u32[]{:S(2)}) collective-permute-start(bf16[256,1536]{1,0:T(8,128)(2,1)S(1)} %pad_maximum_fusion.6), channel_id=1, source_target_pairs={{0,1},{1,2},{2,3},{3,0},{4,5},{5,6},{6,7},{7,4},{8,9},{9,10},{10,1... | collective-permute-start | bytes 2359304 | tf_op jit(solution)/shard_map/ppermute | solution.py:56
  39.2 50.8 %collective-permute-start.6 = (bf16[4,64,1536]{2,1,0:T(8,128)(2,1)S(1)}, bf16[4,64,1536]{2,1,0:T(8,128)(2,1)}, u32[]{:S(2)}, u32[]{:S(2)}) collective-permute-start(bf16[4,64,1536]{2,1,0:T(8,128)(2,1)S(1)} %fusion.14), channel_id=1, source_target_pairs={{0,12},{1,13},{2,14},{3,15},{4,0},{5,1},{6,2},{7,3},{8,4},{9,5},{1... | collective-permute-start | bytes 2359304 | tf_op jit(solution)/shard_map/ppermute | solution.py:56
  42.6 47.5 %collective-permute-start.7 = (bf16[4,64,1536]{2,1,0:T(8,128)(2,1)S(1)}, bf16[4,64,1536]{2,1,0:T(8,128)(2,1)}, u32[]{:S(2)}, u32[]{:S(2)}) collective-permute-start(bf16[4,64,1536]{2,1,0:T(8,128)(2,1)S(1)} %fusion.14), channel_id=1, source_target_pairs={{0,4},{1,5},{2,6},{3,7},{4,8},{5,9},{6,10},{7,11},{8,12},{9,13},{1... | collective-permute-start | bytes 2359304 | tf_op jit(solution)/shard_map/ppermute | solution.py:56
  64.7 18.0 %all-to-all-start.1 = ((bf16[4,3,64,768]{3,2,1,0:T(8,128)(2,1)}), bf16[4,3,64,768]{3,2,1,0:T(8,128)(2,1)S(1)}, u32[]{:S(2)}, u32[]{:S(2)}) async-start(bf16[4,3,64,768]{3,2,1,0:T(8,128)(2,1)} %pad_maximum_fusion.5), calls=%async_computation.1 | async-start | bytes 2359296 | tf_op jit(solution)/shard_map/all_to_all | solution.py:131
  98.9 20.1 %all-to-all-start.3 = ((bf16[4,4,64,768]{3,2,1,0:T(8,128)(2,1)}), bf16[4,4,64,768]{3,2,1,0:T(8,128)(2,1)S(1)}, u32[]{:S(2)}, u32[]{:S(2)}) async-start(bf16[4,4,64,768]{3,2,1,0:T(8,128)(2,1)} %broadcast_in_dim.19), calls=%async_computation.3 | async-start | bytes 3145728 | tf_op jit(solution)/shard_map/all_to_all | solution.py:131
  120.2 19.1 %all-to-all-start.4 = ((bf16[4,4,64,768]{3,2,1,0:T(8,128)(2,1)}), bf16[4,4,64,768]{3,2,1,0:T(8,128)(2,1)S(1)}, u32[]{:S(2)}, u32[]{:S(2)}) async-start(bf16[4,4,64,768]{3,2,1,0:T(8,128)(2,1)} %pad_maximum_fusion.2), calls=%async_computation.4 | async-start | bytes 3145728 | tf_op jit(solution)/shard_map/all_to_all | solution.py:131
  133.4 22.2 %collective-permute-start.14 = (bf16[384,768]{1,0:T(8,128)(2,1)}, bf16[384,768]{1,0:T(8,128)(2,1)}, u32[]{:S(2)}, u32[]{:S(2)}) collective-permute-start(bf16[384,768]{1,0:T(8,128)(2,1)} %convolution_convert_fusion.2), channel_id=1, source_target_pairs={{0,16},{1,17},{2,18},{3,19},{4,20},{5,21},{6,22},{7,23},{8,24},{9,... | collective-permute-start | bytes 1769480 | tf_op jit(solution)/shard_map/ppermute | solution.py:56
  141.3 20.1 %all-to-all-start.5 = ((bf16[4,4,64,768]{3,2,1,0:T(8,128)(2,1)}), bf16[4,4,64,768]{3,2,1,0:T(8,128)(2,1)S(1)}, u32[]{:S(2)}, u32[]{:S(2)}) async-start(bf16[4,4,64,768]{3,2,1,0:T(8,128)(2,1)} %broadcast_in_dim.20), calls=%async_computation.5 | async-start | bytes 3145728 | tf_op jit(solution)/shard_map/all_to_all | solution.py:131
  158.3 24.8 %collective-permute-start.27 = (bf16[384,768]{1,0:T(8,128)(2,1)}, bf16[384,768]{1,0:T(8,128)(2,1)}, u32[]{:S(2)}, u32[]{:S(2)}) collective-permute-start(bf16[384,768]{1,0:T(8,128)(2,1)} %add_convert_fusion.1), channel_id=1, source_target_pairs={{0,128},{1,129},{2,130},{3,131},{4,132},{5,133},{6,134},{7,135},{8... | collective-permute-start | bytes 1769480 | tf_op jit(solution)/shard_map/ppermute | solution.py:56
  160.0 26.2 %collective-permute-start.28 = (bf16[384,768]{1,0:T(8,128)(2,1)}, bf16[384,768]{1,0:T(8,128)(2,1)}, u32[]{:S(2)}, u32[]{:S(2)}) collective-permute-start(bf16[384,768]{1,0:T(8,128)(2,1)} %add_convert_fusion), channel_id=1, source_target_pairs={{0,128},{1,129},{2,130},{3,131},{4,132},{5,133},{6,134},{7,135},{8... | collective-permute-start | bytes 1769480 | tf_op jit(solution)/shard_map/ppermute | solution.py:56
  167.3 25.2 %collective-permute-start.19 = (bf16[384,768]{1,0:T(8,128)(2,1)}, bf16[384,768]{1,0:T(8,128)(2,1)}, u32[]{:S(2)}, u32[]{:S(2)}) collective-permute-start(bf16[384,768]{1,0:T(8,128)(2,1)} %shard_map.93), channel_id=1, source_target_pairs={{0,16},{1,17},{2,18},{3,19},{4,20},{5,21},{6,22},{7,23},{8,24},{9,... | collective-permute-start | bytes 1769480 | tf_op jit(solution)/shard_map/ppermute | solution.py:56
  175.1 17.4 %collective-permute-start.20 = (bf16[400,768]{1,0:T(8,128)(2,1)}, bf16[400,768]{1,0:T(8,128)(2,1)S(1)}, u32[]{:S(2)}, u32[]{:S(2)}) collective-permute-start(bf16[400,768]{1,0:T(8,128)(2,1)} %convolution_convert_fusion), channel_id=1, source_target_pairs={{0,16},{1,17},{2,18},{3,19},{4,20},{5,21},{6,22},{7,23},{8,24},{9,... | collective-permute-start | bytes 1843208 | tf_op jit(solution)/shard_map/ppermute | solution.py:56
  182.3 23.1 %collective-permute-start.16 = (bf16[256,1536]{1,0:T(8,128)(2,1)}, bf16[256,1536]{1,0:T(8,128)(2,1)S(1)}, u32[]{:S(2)}, u32[]{:S(2)}) collective-permute-start(bf16[256,1536]{1,0:T(8,128)(2,1)} %get-tuple-element.54), channel_id=1, source_target_pairs={{0,2},{1,3},{2,0},{3,1},{4,6},{5,7},{6,4},{7,5},{8,10},{9,11},{10,... | collective-permute-start | bytes 2359304 | tf_op jit(solution)/shard_map/ppermute | solution.py:56
  183.1 37.2 %collective-permute-start.17 = (bf16[256,1536]{1,0:T(8,128)(2,1)}, bf16[256,1536]{1,0:T(8,128)(2,1)S(1)}, u32[]{:S(2)}, u32[]{:S(2)}) collective-permute-start(bf16[256,1536]{1,0:T(8,128)(2,1)} %get-tuple-element.55), channel_id=1, source_target_pairs={{0,1},{1,2},{2,3},{3,0},{4,5},{5,6},{6,7},{7,4},{8,9},{9,10},{10,1... | collective-permute-start | bytes 2359304 | tf_op jit(solution)/shard_map/ppermute | solution.py:56
  186.2 34.1 %collective-permute-start.18 = (bf16[256,1536]{1,0:T(8,128)(2,1)}, bf16[256,1536]{1,0:T(8,128)(2,1)}, u32[]{:S(2)}, u32[]{:S(2)}) collective-permute-start(bf16[256,1536]{1,0:T(8,128)(2,1)} %get-tuple-element.56), channel_id=1, source_target_pairs={{0,3},{1,0},{2,1},{3,2},{4,7},{5,4},{6,5},{7,6},{8,11},{9,8},{10,9... | collective-permute-start | bytes 2359304 | tf_op jit(solution)/shard_map/ppermute | solution.py:56
  197.6 30.2 %collective-permute-start.24 = (bf16[384,768]{1,0:T(8,128)(2,1)}, bf16[384,768]{1,0:T(8,128)(2,1)}, u32[]{:S(2)}, u32[]{:S(2)}) collective-permute-start(bf16[384,768]{1,0:T(8,128)(2,1)} %shard_map.95), channel_id=1, source_target_pairs={{0,128},{1,129},{2,130},{3,131},{4,132},{5,133},{6,134},{7,135},{8... | collective-permute-start | bytes 1769480 | tf_op jit(solution)/shard_map/ppermute | solution.py:56
  204.0 39.3 %collective-permute-start.25 = (bf16[400,768]{1,0:T(8,128)(2,1)S(1)}, bf16[400,768]{1,0:T(8,128)(2,1)S(1)}, u32[]{:S(2)}, u32[]{:S(2)}) collective-permute-start(bf16[400,768]{1,0:T(8,128)(2,1)S(1)} %pad_maximum_fusion.11), channel_id=1, source_target_pairs={{0,128},{1,129},{2,130},{3,131},{4,132},{5,133},{6,134},{7,135},{8... | collective-permute-start | bytes 1843208 | tf_op jit(solution)/shard_map/ppermute | solution.py:56
  222.1 18.5 %collective-permute-start.22 = (bf16[64,1536]{1,0:T(8,128)(2,1)S(1)}, bf16[64,1536]{1,0:T(8,128)(2,1)S(1)}, u32[]{:S(2)}, u32[]{:S(2)}) collective-permute-start(bf16[64,1536]{1,0:T(8,128)(2,1)S(1)} %get-tuple-element.71), channel_id=1, source_target_pairs={{0,8},{1,9},{2,10},{3,11},{4,12},{5,13},{6,14},{7,15},{8,0},{9,1},... | collective-permute-start | bytes 589832 | tf_op jit(solution)/shard_map/ppermute | solution.py:56
  (61 other events, 401.8 us)
where the time goes:
time: 249 us; the launch traced here: 247 us
  starting transfers between devices  79.3 us (32%)
  waiting for transfers between devices  62.2 us (25%)
  local copies, waits for them, and re-layouts  32 us (13%)
  other arithmetic  26.8 us (11%)
  matrix products  25.6 us (10%)
  Pallas kernels  19.9 us (8%)
    ppermute x29, starting transfers between devices, send(): return lax.ppermute(value, AXES, pairs)  55.3 us
    ppermute x29, waiting for transfers between devices, send(): return lax.ppermute(value, AXES, pairs)  52.8 us
    dot_general x13, matrix products, dot(): lax.dot_general(a, b, ((contract[:1], contract[1:]), ((), ())), preferred...  25.6 us
    all_to_all x5, starting transfers between devices, swap_x(): lax.all_to_all(value, 'row', 0, 0, tiled=True, axis_index_groups=X_SETS)  19.8 us
    pallas_call x3, Pallas kernels, columns_by(): pl.pallas_call(columns_kernel, grid=(rows // tile,), in_specs=[pl.BlockSp...  12.7 us
    all_to_all x5, waiting for transfers between devices, swap_x(): lax.all_to_all(value, 'row', 0, 0, tiled=True, axis_index_groups=X_SETS)  9.43 us
    pallas_call x1, Pallas kernels, all_shares(): pl.pallas_call(share_kernel, grid=(wide // tile,), in_specs=[pl.BlockSpec...  7.16 us
    unnamed x103, local copies, waits for them, and re-layouts  6.58 us
  transfers between devices with their start and end apart: 35, of which 13 were waited for; matrix products, arithmetic and copies ran while one was open for 30% of the time, Pallas kernels for 8%

commit v1 on v0

--- a/solution.py
+++ b/solution.py
@@ -10,13 +10,30 @@
 coeff = 0.7978845608028654
 
 
-def sincos(positions, first, width):
-    places = positions.astype(jnp.float32)[:, None]
+def add_table_kernel(place_ref, freq_ref, normed_ref, out_ref):
+    angle = place_ref[...] * freq_ref[...]
+    even = lax.broadcasted_iota(jnp.int32, angle.shape, 1) % 2 == 0
+    table = jnp.where(even, jnp.sin(angle), jnp.cos(angle))
+    out_ref[...] = (normed_ref[...].astype(jnp.float32) + table).astype(out_ref.dtype)
+
+
+def add_table(normed, positions, first):
+    rows, width = normed.shape
     column = first + jnp.arange(width, dtype=jnp.int32)
     expo = (2 * (column // 2)).astype(jnp.float32) / jnp.float32(D)
     freq = jnp.power(jnp.float32(10000.0), -expo)
-    angle = places * freq[None, :]
-    return jnp.where((column % 2 == 0)[None, :], jnp.sin(angle), jnp.cos(angle))
+    tile = 16
+    return pl.pallas_call(
+        add_table_kernel,
+        grid=(rows // tile,),
+        in_specs=[
+            pl.BlockSpec((tile, 1), lambda n: (n, 0)),
+            pl.BlockSpec((1, width), lambda n: (0, 0)),
+            pl.BlockSpec((tile, width), lambda n: (n, 0)),
+        ],
+        out_specs=pl.BlockSpec((tile, width), lambda n: (n, 0)),
+        out_shape=jax.ShapeDtypeStruct(normed.shape, normed.dtype),
+    )(positions.astype(jnp.float32)[:, None], freq[None, :], normed)
 
 
 def gelu_pair(value):
@@ -88,34 +105,6 @@
     )(d_pre, w)
 
 
-def columns_kernel(a_ref, b_ref, *refs):
-    product = lax.dot_general(
-        a_ref[...], b_ref[...], (((0,), (0,)), ((), ())), preferred_element_type=jnp.float32
-    )
-    for got_ref in refs[:-1]:
-        product = product + got_ref[...].astype(jnp.float32)
-    refs[-1][...] = product.astype(refs[-1].dtype)
-
-
-def columns_by(a, b, *got):
-    tile = 128
-    rows, size = a.shape[1], b.shape[1]
-    return pl.pallas_call(
-        columns_kernel,
-        grid=(rows // tile,),
-        in_specs=[
-            pl.BlockSpec((a.shape[0], tile), lambda n: (0, n)),
-            pl.BlockSpec(b.shape, lambda n: (0, 0)),
-            *[pl.BlockSpec((tile, size), lambda n: (n, 0))] * len(got),
-        ],
-        out_specs=pl.BlockSpec((tile, size), lambda n: (n, 0)),
-        out_shape=jax.ShapeDtypeStruct((rows, size), a.dtype),
-        cost_estimate=pl.CostEstimate(
-            flops=2 * a.size * size, bytes_accessed=2 * (a.size + b.size + 2 * rows * size), transcendentals=0
-        ),
-    )(a, b, *got)
-
-
 def on_device(normed, positions, cotangent, w_in, b_in, w_out):
     bf, f32 = jnp.bfloat16, jnp.float32
     width = w_in.shape[0]
@@ -136,7 +125,7 @@
     def gather_x(own):
         return swap_x(jnp.broadcast_to(own[None], (4,) + own.shape))
 
-    inputs = (normed.astype(f32) + sincos(positions, row * width, width)).astype(bf)
+    inputs = add_table(normed, positions, row * width)
     both = jnp.stack([inputs, cotangent])
     mine = lax.dynamic_slice_in_dim(both, core * half, half, 1)
     other = send(lax.dynamic_slice_in_dim(both, (1 - core) * half, half, 1), CORE)
@@ -200,19 +189,18 @@
     d_raw = after(d_pre_all, x_mine, x_other)
     d_pre_all = d_raw.swapaxes(0, 1)
     d_pre_rows = d_pre_all.reshape(-1, hidden)
-    d_pre_rows = after(d_pre_rows, out_mine)
-    in_other = [columns_by(x_other[0], d_pre_rows), dot(x_other[1], d_pre_rows, (0, 0), bf)]
+    in_other = [dot(x, after(d_pre_rows, out_mine), (0, 0), bf) for x in x_other]
     in_got = [send(other, CORE) for other in in_other]
     *shares, total = all_shares(after(d_raw, in_other), w_in_all)
     got = [send(share, Y_BY[k]) for share, k in zip(shares, (2, 1, 3))]
     in_got = after(in_got, *shares)
     out_deep = after(out_deep, *shares)
-    d_w_out = jnp.concatenate([mine.astype(f32) + deep.astype(f32) for mine, deep in zip(out_mine, out_deep)])
-    in_mine = [columns_by(x, d_pre_rows, got) for x, got in zip(x_mine, in_got)]
+    d_w_out = jnp.concatenate(out_mine).astype(f32) + jnp.concatenate(out_deep).astype(f32)
+    in_mine = [(dot(x, d_pre_rows, (0, 0)) + got[:cut].astype(f32)).astype(bf) for x, got in zip(x_mine, in_got)]
     bias = (in_other[1][cut:].astype(f32) + in_got[1][cut:].astype(f32)).astype(bf)
     in_both = [in_mine[0], jnp.concatenate([in_mine[1], bias])]
     in_deep = [send(mine, DEPTH) for mine in in_both]
-    d_w_in = jnp.concatenate([mine.astype(f32) + deep[:cut].astype(f32) for mine, deep in zip(in_mine, in_deep)])
+    d_w_in = jnp.concatenate(in_mine).astype(f32) + jnp.concatenate([deep[:cut] for deep in in_deep]).astype(f32)
 
     for term in after(got, in_both):
         total = total + term.astype(f32)

time: 249 us -> 246 us (0.988)
  waiting for transfers between devices: 62.2 us -> 79.6 us
  other arithmetic: 26.8 us -> 16.3 us
  Pallas kernels: 19.9 us -> 12.5 us
  matrix products: 25.6 us -> 30.5 us
  starting transfers between devices: 79.3 us -> 75.1 us
  local copies, waits for them, and re-layouts: 32 us -> 29.3 us
    ppermute x29, waiting for transfers between devices: 52.8 us -> 61.6 us  [send(): return lax.ppermute(value, AXES, pairs)]
    all_to_all x5, waiting for transfers between devices: 9.43 us -> 18 us  [swap_x(): lax.all_to_all(value, 'row', 0, 0, tiled=True, axis_index_groups=X_SETS)]
    pallas_call x3 -> x1, Pallas kernels: 12.7 us -> 5.3 us  [add_table(): pl.pallas_call(add_table_kernel, grid=(rows // tile,), in_specs=[pl.Block...]
    dot_general x13 -> x16, matrix products: 25.6 us -> 30.5 us  [dot(): lax.dot_general(a, b, ((contract[:1], contract[1:]), ((), ())), preferred...]
    concatenate x4 -> x1, other arithmetic: 5.28 us -> 1.05 us  [on_device(): jnp.concatenate([x[:, i * cut:(i + 1) * cut] for x in xs])]
    ppermute x29, starting transfers between devices: 55.3 us -> 51.6 us  [send(): return lax.ppermute(value, AXES, pairs)]
    concatenate x2 -> x0, other arithmetic: 3.12 us -> none  [the longest x1 1.56 us: on_device(): jnp.concatenate([mine.astype(f32) + deep.astype(f32) for mine, deep in zi...]
    unnamed x103 -> x93, local copies, waits for them, and re-layouts: 6.58 us -> 7.41 us
  transfers between devices with their start and end apart: 35 -> 35, of which waited for: 13 -> 15; matrix products, arithmetic and copies ran while one was open for 30% -> 28% of each run, Pallas kernels for 8% -> 3%
where the time goes in v1:
time: 246 us; the launch traced here: 245 us
  waiting for transfers between devices  79.6 us (32%)
  starting transfers between devices  75.1 us (31%)
  matrix products  30.5 us (12%)
  local copies, waits for them, and re-layouts  29.3 us (12%)
  other arithmetic  16.3 us (7%)
  Pallas kernels  12.5 us (5%)
    ppermute x29, waiting for transfers between devices, send(): return lax.ppermute(value, AXES, pairs)  61.6 us
    ppermute x29, starting transfers between devices, send(): return lax.ppermute(value, AXES, pairs)  51.6 us
    dot_general x16, matrix products, dot(): lax.dot_general(a, b, ((contract[:1], contract[1:]), ((), ())), preferred...  30.5 us
    all_to_all x5, starting transfers between devices, swap_x(): lax.all_to_all(value, 'row', 0, 0, tiled=True, axis_index_groups=X_SETS)  19.3 us
    all_to_all x5, waiting for transfers between devices, swap_x(): lax.all_to_all(value, 'row', 0, 0, tiled=True, axis_index_groups=X_SETS)  18 us
    unnamed x93, local copies, waits for them, and re-layouts  7.41 us
    pallas_call x1, Pallas kernels, all_shares(): pl.pallas_call(share_kernel, grid=(wide // tile,), in_specs=[pl.BlockSpec...  7.21 us
    pallas_call x1, Pallas kernels, add_table(): pl.pallas_call(add_table_kernel, grid=(rows // tile,), in_specs=[pl.Block...  5.3 us
  transfers between devices with their start and end apart: 35, of which 15 were waited for; matrix products, arithmetic and copies ran while one was open for 28% of the time, Pallas kernels for 3%

profile of v1, /device:TPU:1, one launch (start us, length us, event | category | flops | bytes accessed | tf_op | source)
XLA Modules:
  0.0 244.6 jit_solution(17593466442435234485)
XLA Ops:
  2.8 5.3 %shard_map.93 = bf16[128,768]{1,0:T(8,128)(2,1)} custom-call(f32[128,1]{1,0:T(8,128)} %copy.13.place_ref, f32[1,768]{1,0:T(1,128)} %negate_power_fusion.freq_ref, bf16[128,768]{1,0:T(8,128)(2,1)} %normed_ref.1), custom_call_target="tpu_custom_call" | custom-call | tf_op jit(solution)/shard_map/pallas_call | solution.py:26
  9.1 3.3 %collective-permute-start = (bf16[2,64,768]{2,1,0:T(8,128)(2,1)S(1)}, bf16[2,64,768]{2,1,0:T(8,128)(2,1)S(1)}, u32[]{:S(2)}, u32[]{:S(2)}) collective-permute-start(bf16[2,64,768]{2,1,0:T(8,128)(2,1)S(1)} %get-tuple-element.98), channel_id=1, source_target_pairs={{0,16},{1,17},{2,18},{3,19},{4,20},{5,21},{6,22},{7,23},{8,24},{9,... | collective-permute-start | bytes 589832 | tf_op jit(solution)/shard_map/ppermute | solution.py:73
  15.5 5.1 %collective-permute-start.2 = (bf16[64,1536]{1,0:T(8,128)(2,1)S(1)}, bf16[64,1536]{1,0:T(8,128)(2,1)S(1)}, u32[]{:S(2)}, u32[]{:S(2)}) collective-permute-start(bf16[64,1536]{1,0:T(8,128)(2,1)S(1)} %pad_maximum_fusion.15), channel_id=1, source_target_pairs={{0,8},{1,9},{2,10},{3,11},{4,12},{5,13},{6,14},{7,15},{8,0},{9,1},... | collective-permute-start | bytes 589832 | tf_op jit(solution)/shard_map/ppermute | solution.py:73
  24.0 4.2 %all-to-all-start = ((bf16[4,64,1536]{2,1,0:T(8,128)(2,1)}), bf16[4,64,1536]{2,1,0:T(8,128)(2,1)S(1)}, u32[]{:S(2)}, u32[]{:S(2)}) async-start(bf16[4,64,1536]{2,1,0:T(8,128)(2,1)} %broadcast_in_dim.11), calls=%async_computation | async-start | bytes 1572864 | tf_op jit(solution)/shard_map/all_to_all | solution.py:141
  29.2 3.5 %collective-permute-done.2 = bf16[64,1536]{1,0:T(8,128)(2,1)S(1)} collective-permute-done((bf16[64,1536]{1,0:T(8,128)(2,1)S(1)}, bf16[64,1536]{1,0:T(8,128)(2,1)S(1)}, u32[]{:S(2)}, u32[]{:S(2)}) %collective-permute-start.2) | collective-permute-done | bytes 196640 | tf_op jit(solution)/shard_map/ppermute | solution.py:73
  32.8 6.5 %collective-permute-done.1 = bf16[64,1536]{1,0:T(8,128)(2,1)S(1)} collective-permute-done((bf16[64,1536]{1,0:T(8,128)(2,1)S(1)}, bf16[64,1536]{1,0:T(8,128)(2,1)S(1)}, u32[]{:S(2)}, u32[]{:S(2)}) %collective-permute-start.1) | collective-permute-done | bytes 196640 | tf_op jit(solution)/shard_map/ppermute | solution.py:73
  44.1 3.4 %collective-permute-start.6 = (bf16[4,64,1536]{2,1,0:T(8,128)(2,1)S(1)}, bf16[4,64,1536]{2,1,0:T(8,128)(2,1)}, u32[]{:S(2)}, u32[]{:S(2)}) collective-permute-start(bf16[4,64,1536]{2,1,0:T(8,128)(2,1)S(1)} %fusion.14), channel_id=1, source_target_pairs={{0,12},{1,13},{2,14},{3,15},{4,0},{5,1},{6,2},{7,3},{8,4},{9,5},{1... | collective-permute-start | bytes 2359304 | tf_op jit(solution)/shard_map/ppermute | solution.py:73
  52.4 6.8 %collective-permute-done.8 = bf16[256,1536]{1,0:T(8,128)(2,1)S(1)} collective-permute-done((bf16[256,1536]{1,0:T(8,128)(2,1)S(1)}, bf16[256,1536]{1,0:T(8,128)(2,1)S(1)}, u32[]{:S(2)}, u32[]{:S(2)}) %collective-permute-start.8) | collective-permute-done | bytes 786464 | tf_op jit(solution)/shard_map/ppermute | solution.py:73
  69.6 4.0 %all-to-all-start.1 = ((bf16[4,3,64,768]{3,2,1,0:T(8,128)(2,1)}), bf16[4,3,64,768]{3,2,1,0:T(8,128)(2,1)S(1)}, u32[]{:S(2)}, u32[]{:S(2)}) async-start(bf16[4,3,64,768]{3,2,1,0:T(8,128)(2,1)} %pad_maximum_fusion.3), calls=%async_computation.1 | async-start | bytes 2359296 | tf_op jit(solution)/shard_map/all_to_all | solution.py:120
  81.6 6.0 %all-to-all-done.1 = bf16[4,3,64,768]{3,2,1,0:T(8,128)(2,1)S(1)} async-done(((bf16[4,3,64,768]{3,2,1,0:T(8,128)(2,1)}), bf16[4,3,64,768]{3,2,1,0:T(8,128)(2,1)S(1)}, u32[]{:S(2)}, u32[]{:S(2)}) %all-to-all-start.1) | async-done | bytes 1179680 | tf_op jit(solution)/shard_map/all_to_all | solution.py:120
  87.8 3.5 %all-to-all-start.2 = ((bf16[4,1,64,768]{3,2,1,0:T(8,128)(2,1)}), bf16[4,1,64,768]{3,2,1,0:T(8,128)(2,1)S(1)}, u32[]{:S(2)}, u32[]{:S(2)}) async-start(bf16[4,1,64,768]{3,2,1,0:T(8,128)(2,1)} %bitcast.22), calls=%async_computation.2 | async-start | bytes 786432 | tf_op jit(solution)/shard_map/all_to_all | solution.py:120
  102.1 4.2 %all-to-all-start.3 = ((bf16[4,4,64,768]{3,2,1,0:T(8,128)(2,1)}), bf16[4,4,64,768]{3,2,1,0:T(8,128)(2,1)S(1)}, u32[]{:S(2)}, u32[]{:S(2)}) async-start(bf16[4,4,64,768]{3,2,1,0:T(8,128)(2,1)} %broadcast_in_dim.13), calls=%async_computation.3 | async-start | bytes 3145728 | tf_op jit(solution)/shard_map/all_to_all | solution.py:120
  116.4 5.7 %all-to-all-done.3 = bf16[4,4,64,768]{3,2,1,0:T(8,128)(2,1)S(1)} async-done(((bf16[4,4,64,768]{3,2,1,0:T(8,128)(2,1)}), bf16[4,4,64,768]{3,2,1,0:T(8,128)(2,1)S(1)}, u32[]{:S(2)}, u32[]{:S(2)}) %all-to-all-start.3) | async-done | bytes 1572896 | tf_op jit(solution)/shard_map/all_to_all | solution.py:120
  123.3 3.6 %all-to-all-start.4 = ((bf16[4,4,64,768]{3,2,1,0:T(8,128)(2,1)}), bf16[4,4,64,768]{3,2,1,0:T(8,128)(2,1)S(1)}, u32[]{:S(2)}, u32[]{:S(2)}) async-start(bf16[4,4,64,768]{3,2,1,0:T(8,128)(2,1)} %pad_maximum_fusion), calls=%async_computation.4 | async-start | bytes 3145728 | tf_op jit(solution)/shard_map/all_to_all | solution.py:120
  132.8 5.8 %collective-permute-start.14 = (bf16[384,768]{1,0:T(8,128)(2,1)}, bf16[384,768]{1,0:T(8,128)(2,1)}, u32[]{:S(2)}, u32[]{:S(2)}) collective-permute-start(bf16[384,768]{1,0:T(8,128)(2,1)} %convolution_convert_fusion.3), channel_id=1, source_target_pairs={{0,16},{1,17},{2,18},{3,19},{4,20},{5,21},{6,22},{7,23},{8,24},{9,... | collective-permute-start | bytes 1769480 | tf_op jit(solution)/shard_map/ppermute | solution.py:73
  143.6 4.0 %all-to-all-start.5 = ((bf16[4,4,64,768]{3,2,1,0:T(8,128)(2,1)}), bf16[4,4,64,768]{3,2,1,0:T(8,128)(2,1)S(1)}, u32[]{:S(2)}, u32[]{:S(2)}) async-start(bf16[4,4,64,768]{3,2,1,0:T(8,128)(2,1)} %broadcast_in_dim.14), calls=%async_computation.5 | async-start | bytes 3145728 | tf_op jit(solution)/shard_map/all_to_all | solution.py:120
  156.6 4.9 %all-to-all-done.5.d_ref = bf16[4,4,64,768]{3,2,1,0:T(8,128)(2,1)S(1)} async-done(((bf16[4,4,64,768]{3,2,1,0:T(8,128)(2,1)}), bf16[4,4,64,768]{3,2,1,0:T(8,128)(2,1)S(1)}, u32[]{:S(2)}, u32[]{:S(2)}) %all-to-all-start.5) | async-done | bytes 1572896 | tf_op jit(solution)/shard_map/all_to_all | solution.py:120
  165.0 7.9 %collective-permute-start.20 = (bf16[400,768]{1,0:T(8,128)(2,1)}, bf16[400,768]{1,0:T(8,128)(2,1)S(1)}, u32[]{:S(2)}, u32[]{:S(2)}) collective-permute-start(bf16[400,768]{1,0:T(8,128)(2,1)} %convolution_convert_fusion), channel_id=1, source_target_pairs={{0,16},{1,17},{2,18},{3,19},{4,20},{5,21},{6,22},{7,23},{8,24},{9,... | collective-permute-start | bytes 1843208 | tf_op jit(solution)/shard_map/ppermute | solution.py:73
  174.6 7.2 %shard_map.94 = (bf16[256,1536]{1,0:T(8,128)(2,1)}, bf16[256,1536]{1,0:T(8,128)(2,1)}, bf16[256,1536]{1,0:T(8,128)(2,1)}, f32[256,1536]{1,0:T(8,128)}) custom-call(bf16[4,4,64,768]{3,2,1,0:T(8,128)(2,1)} %copy-done, bf16[1536,768]{1,0:T(8,128)(2,1)} %constant_dynamic-update-slice_fusion.2.w_ref), custom_call_target="tpu_custom_call" | custom-call | flops 2415919104 | bytes 7864320 | tf_op jit(solution)/shard_map/pallas_call | solution.py:93
  191.3 10.8 %collective-permute-done.16 = bf16[256,1536]{1,0:T(8,128)(2,1)S(1)} collective-permute-done((bf16[256,1536]{1,0:T(8,128)(2,1)}, bf16[256,1536]{1,0:T(8,128)(2,1)S(1)}, u32[]{:S(2)}, u32[]{:S(2)}) %collective-permute-start.16) | collective-permute-done | bytes 786464 | tf_op jit(solution)/shard_map/ppermute | solution.py:73
  202.2 17.7 %collective-permute-done.17 = bf16[256,1536]{1,0:T(8,128)(2,1)S(1)} collective-permute-done((bf16[256,1536]{1,0:T(8,128)(2,1)}, bf16[256,1536]{1,0:T(8,128)(2,1)S(1)}, u32[]{:S(2)}, u32[]{:S(2)}) %collective-permute-start.17) | collective-permute-done | bytes 786464 | tf_op jit(solution)/shard_map/ppermute | solution.py:73
  220.5 4.0 %collective-permute-start.22 = (bf16[64,1536]{1,0:T(8,128)(2,1)S(1)}, bf16[64,1536]{1,0:T(8,128)(2,1)S(1)}, u32[]{:S(2)}, u32[]{:S(2)}) collective-permute-start(bf16[64,1536]{1,0:T(8,128)(2,1)S(1)} %get-tuple-element.71), channel_id=1, source_target_pairs={{0,8},{1,9},{2,10},{3,11},{4,12},{5,13},{6,14},{7,15},{8,0},{9,1},... | collective-permute-start | bytes 589832 | tf_op jit(solution)/shard_map/ppermute | solution.py:73
  226.2 3.3 %convert_add_fusion = f32[768,768]{1,0:T(8,128)} fusion(bf16[384,768]{1,0:T(8,128)(2,1)} %add_convert_fusion.2, bf16[384,768]{1,0:T(8,128)(2,1)} %add_convert_fusion.3, bf16[384,768]{1,0:T(8,128)(2,1)} %collective-permute-done.28, bf16[384,768]{1,0:T(8,128)(2,1)} %collective-permute-done.27), kind=kLoop, calls=%fused_computation.1 | loop fusion | flops 5308416 | bytes 4718592 | tf_op jit(solution)/shard_map/add | solution.py:198
  230.1 9.5 %collective-permute-done.22 = bf16[64,1536]{1,0:T(8,128)(2,1)S(1)} collective-permute-done((bf16[64,1536]{1,0:T(8,128)(2,1)S(1)}, bf16[64,1536]{1,0:T(8,128)(2,1)S(1)}, u32[]{:S(2)}, u32[]{:S(2)}) %collective-permute-start.22) | collective-permute-done | bytes 196640 | tf_op jit(solution)/shard_map/ppermute | solution.py:73
  (208 shorter events, 103.4 us)
Async XLA Ops:
  12.5 31.6 %collective-permute-start.4 = (bf16[768,768]{1,0:T(8,128)(2,1)}, bf16[768,768]{1,0:T(8,128)(2,1)}, u32[]{:S(2)}, u32[]{:S(2)}) collective-permute-start(bf16[768,768]{1,0:T(8,128)(2,1)} %param.9), channel_id=1, source_target_pairs={{0,16},{1,17},{2,18},{3,19},{4,20},{5,21},{6,22},{7,23},{8,24},{9,... | collective-permute-start | bytes 3538952 | tf_op jit(solution)/shard_map/ppermute | solution.py:73
  12.6 31.5 %collective-permute-start.5 = (bf16[768,768]{1,0:T(8,128)(2,1)}, bf16[768,768]{1,0:T(8,128)(2,1)}, u32[]{:S(2)}, u32[]{:S(2)}) collective-permute-start(bf16[768,768]{1,0:T(8,128)(2,1)} %param.11), channel_id=1, source_target_pairs={{0,16},{1,17},{2,18},{3,19},{4,20},{5,21},{6,22},{7,23},{8,24},{9,... | collective-permute-start | bytes 3538952 | tf_op jit(solution)/shard_map/ppermute | solution.py:73
  15.5 17.2 %collective-permute-start.2 = (bf16[64,1536]{1,0:T(8,128)(2,1)S(1)}, bf16[64,1536]{1,0:T(8,128)(2,1)S(1)}, u32[]{:S(2)}, u32[]{:S(2)}) collective-permute-start(bf16[64,1536]{1,0:T(8,128)(2,1)S(1)} %pad_maximum_fusion.15), channel_id=1, source_target_pairs={{0,8},{1,9},{2,10},{3,11},{4,12},{5,13},{6,14},{7,15},{8,0},{9,1},... | collective-permute-start | bytes 589832 | tf_op jit(solution)/shard_map/ppermute | solution.py:73
  20.6 18.6 %collective-permute-start.1 = (bf16[64,1536]{1,0:T(8,128)(2,1)S(1)}, bf16[64,1536]{1,0:T(8,128)(2,1)S(1)}, u32[]{:S(2)}, u32[]{:S(2)}) collective-permute-start(bf16[64,1536]{1,0:T(8,128)(2,1)S(1)} %pad_maximum_fusion.15), channel_id=1, source_target_pairs={{0,12},{1,13},{2,14},{3,15},{4,0},{5,1},{6,2},{7,3},{8,4},{9,5},{1... | collective-permute-start | bytes 589832 | tf_op jit(solution)/shard_map/ppermute | solution.py:73
  24.0 19.8 %all-to-all-start = ((bf16[4,64,1536]{2,1,0:T(8,128)(2,1)}), bf16[4,64,1536]{2,1,0:T(8,128)(2,1)S(1)}, u32[]{:S(2)}, u32[]{:S(2)}) async-start(bf16[4,64,1536]{2,1,0:T(8,128)(2,1)} %broadcast_in_dim.11), calls=%async_computation | async-start | bytes 1572864 | tf_op jit(solution)/shard_map/all_to_all | solution.py:141
  40.0 19.2 %collective-permute-start.8 = (bf16[256,1536]{1,0:T(8,128)(2,1)S(1)}, bf16[256,1536]{1,0:T(8,128)(2,1)S(1)}, u32[]{:S(2)}, u32[]{:S(2)}) collective-permute-start(bf16[256,1536]{1,0:T(8,128)(2,1)S(1)} %pad_maximum_fusion.4), channel_id=1, source_target_pairs={{0,3},{1,0},{2,1},{3,2},{4,7},{5,4},{6,5},{7,6},{8,11},{9,8},{10,9... | collective-permute-start | bytes 2359304 | tf_op jit(solution)/shard_map/ppermute | solution.py:73
  42.8 19.6 %collective-permute-start.9 = (bf16[256,1536]{1,0:T(8,128)(2,1)S(1)}, bf16[256,1536]{1,0:T(8,128)(2,1)}, u32[]{:S(2)}, u32[]{:S(2)}) collective-permute-start(bf16[256,1536]{1,0:T(8,128)(2,1)S(1)} %pad_maximum_fusion.4), channel_id=1, source_target_pairs={{0,1},{1,2},{2,3},{3,0},{4,5},{5,6},{6,7},{7,4},{8,9},{9,10},{10,1... | collective-permute-start | bytes 2359304 | tf_op jit(solution)/shard_map/ppermute | solution.py:73
  44.1 50.5 %collective-permute-start.6 = (bf16[4,64,1536]{2,1,0:T(8,128)(2,1)S(1)}, bf16[4,64,1536]{2,1,0:T(8,128)(2,1)}, u32[]{:S(2)}, u32[]{:S(2)}) collective-permute-start(bf16[4,64,1536]{2,1,0:T(8,128)(2,1)S(1)} %fusion.14), channel_id=1, source_target_pairs={{0,12},{1,13},{2,14},{3,15},{4,0},{5,1},{6,2},{7,3},{8,4},{9,5},{1... | collective-permute-start | bytes 2359304 | tf_op jit(solution)/shard_map/ppermute | solution.py:73
  47.4 47.1 %collective-permute-start.7 = (bf16[4,64,1536]{2,1,0:T(8,128)(2,1)S(1)}, bf16[4,64,1536]{2,1,0:T(8,128)(2,1)}, u32[]{:S(2)}, u32[]{:S(2)}) collective-permute-start(bf16[4,64,1536]{2,1,0:T(8,128)(2,1)S(1)} %fusion.14), channel_id=1, source_target_pairs={{0,4},{1,5},{2,6},{3,7},{4,8},{5,9},{6,10},{7,11},{8,12},{9,13},{1... | collective-permute-start | bytes 2359304 | tf_op jit(solution)/shard_map/ppermute | solution.py:73
  69.6 18.0 %all-to-all-start.1 = ((bf16[4,3,64,768]{3,2,1,0:T(8,128)(2,1)}), bf16[4,3,64,768]{3,2,1,0:T(8,128)(2,1)S(1)}, u32[]{:S(2)}, u32[]{:S(2)}) async-start(bf16[4,3,64,768]{3,2,1,0:T(8,128)(2,1)} %pad_maximum_fusion.3), calls=%async_computation.1 | async-start | bytes 2359296 | tf_op jit(solution)/shard_map/all_to_all | solution.py:120
  95.6 16.8 %collective-permute-start.13 = (bf16[2,64,1536]{2,1,0:T(8,128)(2,1)S(1)}, bf16[2,64,1536]{2,1,0:T(8,128)(2,1)}, u32[]{:S(2)}, u32[]{:S(2)}) collective-permute-start(bf16[2,64,1536]{2,1,0:T(8,128)(2,1)S(1)} %slice.158), channel_id=1, source_target_pairs={{0,4},{1,5},{2,6},{3,7},{4,8},{5,9},{6,10},{7,11},{8,12},{9,13},{1... | collective-permute-start | bytes 1179656 | tf_op jit(solution)/shard_map/ppermute | solution.py:73
  102.1 20.1 %all-to-all-start.3 = ((bf16[4,4,64,768]{3,2,1,0:T(8,128)(2,1)}), bf16[4,4,64,768]{3,2,1,0:T(8,128)(2,1)S(1)}, u32[]{:S(2)}, u32[]{:S(2)}) async-start(bf16[4,4,64,768]{3,2,1,0:T(8,128)(2,1)} %broadcast_in_dim.13), calls=%async_computation.3 | async-start | bytes 3145728 | tf_op jit(solution)/shard_map/all_to_all | solution.py:120
  123.3 18.2 %all-to-all-start.4 = ((bf16[4,4,64,768]{3,2,1,0:T(8,128)(2,1)}), bf16[4,4,64,768]{3,2,1,0:T(8,128)(2,1)S(1)}, u32[]{:S(2)}, u32[]{:S(2)}) async-start(bf16[4,4,64,768]{3,2,1,0:T(8,128)(2,1)} %pad_maximum_fusion), calls=%async_computation.4 | async-start | bytes 3145728 | tf_op jit(solution)/shard_map/all_to_all | solution.py:120
  132.8 16.8 %collective-permute-start.14 = (bf16[384,768]{1,0:T(8,128)(2,1)}, bf16[384,768]{1,0:T(8,128)(2,1)}, u32[]{:S(2)}, u32[]{:S(2)}) collective-permute-start(bf16[384,768]{1,0:T(8,128)(2,1)} %convolution_convert_fusion.3), channel_id=1, source_target_pairs={{0,16},{1,17},{2,18},{3,19},{4,20},{5,21},{6,22},{7,23},{8,24},{9,... | collective-permute-start | bytes 1769480 | tf_op jit(solution)/shard_map/ppermute | solution.py:73
  143.6 17.8 %all-to-all-start.5 = ((bf16[4,4,64,768]{3,2,1,0:T(8,128)(2,1)}), bf16[4,4,64,768]{3,2,1,0:T(8,128)(2,1)S(1)}, u32[]{:S(2)}, u32[]{:S(2)}) async-start(bf16[4,4,64,768]{3,2,1,0:T(8,128)(2,1)} %broadcast_in_dim.14), calls=%async_computation.5 | async-start | bytes 3145728 | tf_op jit(solution)/shard_map/all_to_all | solution.py:120
  152.4 30.9 %collective-permute-start.27 = (bf16[384,768]{1,0:T(8,128)(2,1)}, bf16[384,768]{1,0:T(8,128)(2,1)}, u32[]{:S(2)}, u32[]{:S(2)}) collective-permute-start(bf16[384,768]{1,0:T(8,128)(2,1)} %add_convert_fusion.3), channel_id=1, source_target_pairs={{0,128},{1,129},{2,130},{3,131},{4,132},{5,133},{6,134},{7,135},{8... | collective-permute-start | bytes 1769480 | tf_op jit(solution)/shard_map/ppermute | solution.py:73
  155.1 29.3 %collective-permute-start.28 = (bf16[384,768]{1,0:T(8,128)(2,1)}, bf16[384,768]{1,0:T(8,128)(2,1)}, u32[]{:S(2)}, u32[]{:S(2)}) collective-permute-start(bf16[384,768]{1,0:T(8,128)(2,1)} %add_convert_fusion.2), channel_id=1, source_target_pairs={{0,128},{1,129},{2,130},{3,131},{4,132},{5,133},{6,134},{7,135},{8... | collective-permute-start | bytes 1769480 | tf_op jit(solution)/shard_map/ppermute | solution.py:73
  165.0 21.0 %collective-permute-start.20 = (bf16[400,768]{1,0:T(8,128)(2,1)}, bf16[400,768]{1,0:T(8,128)(2,1)S(1)}, u32[]{:S(2)}, u32[]{:S(2)}) collective-permute-start(bf16[400,768]{1,0:T(8,128)(2,1)} %convolution_convert_fusion), channel_id=1, source_target_pairs={{0,16},{1,17},{2,18},{3,19},{4,20},{5,21},{6,22},{7,23},{8,24},{9,... | collective-permute-start | bytes 1843208 | tf_op jit(solution)/shard_map/ppermute | solution.py:73
  181.8 20.4 %collective-permute-start.16 = (bf16[256,1536]{1,0:T(8,128)(2,1)}, bf16[256,1536]{1,0:T(8,128)(2,1)S(1)}, u32[]{:S(2)}, u32[]{:S(2)}) collective-permute-start(bf16[256,1536]{1,0:T(8,128)(2,1)} %get-tuple-element.54), channel_id=1, source_target_pairs={{0,2},{1,3},{2,0},{3,1},{4,6},{5,7},{6,4},{7,5},{8,10},{9,11},{10,... | collective-permute-start | bytes 2359304 | tf_op jit(solution)/shard_map/ppermute | solution.py:73
  183.3 36.5 %collective-permute-start.17 = (bf16[256,1536]{1,0:T(8,128)(2,1)}, bf16[256,1536]{1,0:T(8,128)(2,1)S(1)}, u32[]{:S(2)}, u32[]{:S(2)}) collective-permute-start(bf16[256,1536]{1,0:T(8,128)(2,1)} %get-tuple-element.55), channel_id=1, source_target_pairs={{0,1},{1,2},{2,3},{3,0},{4,5},{5,6},{6,7},{7,4},{8,9},{9,10},{10,1... | collective-permute-start | bytes 2359304 | tf_op jit(solution)/shard_map/ppermute | solution.py:73
  184.4 35.4 %collective-permute-start.18 = (bf16[256,1536]{1,0:T(8,128)(2,1)}, bf16[256,1536]{1,0:T(8,128)(2,1)S(1)}, u32[]{:S(2)}, u32[]{:S(2)}) collective-permute-start(bf16[256,1536]{1,0:T(8,128)(2,1)} %get-tuple-element.56), channel_id=1, source_target_pairs={{0,3},{1,0},{2,1},{3,2},{4,7},{5,4},{6,5},{7,6},{8,11},{9,8},{10,9... | collective-permute-start | bytes 2359304 | tf_op jit(solution)/shard_map/ppermute | solution.py:73
  188.0 52.8 %collective-permute-start.24 = (bf16[384,768]{1,0:T(8,128)(2,1)S(1)}, bf16[384,768]{1,0:T(8,128)(2,1)S(1)}, u32[]{:S(2)}, u32[]{:S(2)}) collective-permute-start(bf16[384,768]{1,0:T(8,128)(2,1)S(1)} %add_convert_fusion.1), channel_id=1, source_target_pairs={{0,128},{1,129},{2,130},{3,131},{4,132},{5,133},{6,134},{7,135},{8... | collective-permute-start | bytes 1769480 | tf_op jit(solution)/shard_map/ppermute | solution.py:73
  189.8 51.1 %collective-permute-start.25 = (bf16[400,768]{1,0:T(8,128)(2,1)S(1)}, bf16[400,768]{1,0:T(8,128)(2,1)S(1)}, u32[]{:S(2)}, u32[]{:S(2)}) collective-permute-start(bf16[400,768]{1,0:T(8,128)(2,1)S(1)} %pad_maximum_fusion.9), channel_id=1, source_target_pairs={{0,128},{1,129},{2,130},{3,131},{4,132},{5,133},{6,134},{7,135},{8... | collective-permute-start | bytes 1843208 | tf_op jit(solution)/shard_map/ppermute | solution.py:73
  220.5 19.1 %collective-permute-start.22 = (bf16[64,1536]{1,0:T(8,128)(2,1)S(1)}, bf16[64,1536]{1,0:T(8,128)(2,1)S(1)}, u32[]{:S(2)}, u32[]{:S(2)}) collective-permute-start(bf16[64,1536]{1,0:T(8,128)(2,1)S(1)} %get-tuple-element.71), channel_id=1, source_target_pairs={{0,8},{1,9},{2,10},{3,11},{4,12},{5,13},{6,14},{7,15},{8,0},{9,1},... | collective-permute-start | bytes 589832 | tf_op jit(solution)/shard_map/ppermute | solution.py:73
  (56 other events, 414.9 us)

commit v2 on v1

--- a/solution.py
+++ b/solution.py
@@ -187,11 +187,11 @@
     x_other = [jnp.concatenate([x[:, i * cut : (i + 1) * cut] for x in xs]) for i in (2, 3)]
     x_other[1] = jnp.concatenate([x_other[1], jnp.ones((x_other[1].shape[0], 16), bf)], axis=1)
     d_raw = after(d_pre_all, x_mine, x_other)
-    d_pre_all = d_raw.swapaxes(0, 1)
+    *shares, total = all_shares(d_raw, w_in_all)
+    d_pre_all = after(d_raw, *shares).swapaxes(0, 1)
     d_pre_rows = d_pre_all.reshape(-1, hidden)
     in_other = [dot(x, after(d_pre_rows, out_mine), (0, 0), bf) for x in x_other]
     in_got = [send(other, CORE) for other in in_other]
-    *shares, total = all_shares(after(d_raw, in_other), w_in_all)
     got = [send(share, Y_BY[k]) for share, k in zip(shares, (2, 1, 3))]
     in_got = after(in_got, *shares)
     out_deep = after(out_deep, *shares)

time: 246 us -> 260 us (1.057)
  the two profiles are of different devices: /device:TPU:1 before, /device:TPU:33 now
where the time goes in v2:
time: 260 us; the launch traced here: 258 us
  waiting for transfers between devices  108 us (42%)
  starting transfers between devices  62.1 us (24%)
  matrix products  30.8 us (12%)
  local copies, waits for them, and re-layouts  28.1 us (11%)
  other arithmetic  15 us (6%)
  Pallas kernels  12.5 us (5%)
    ppermute x29, waiting for transfers between devices, send(): return lax.ppermute(value, AXES, pairs)  76.3 us
    ppermute x29, starting transfers between devices, send(): return lax.ppermute(value, AXES, pairs)  39.2 us
    all_to_all x5, waiting for transfers between devices, swap_x(): lax.all_to_all(value, 'row', 0, 0, tiled=True, axis_index_groups=X_SETS)  31.6 us
    dot_general x16, matrix products, dot(): lax.dot_general(a, b, ((contract[:1], contract[1:]), ((), ())), preferred...  30.8 us
    all_to_all x5, starting transfers between devices, swap_x(): lax.all_to_all(value, 'row', 0, 0, tiled=True, axis_index_groups=X_SETS)  18.8 us
    pallas_call x1, Pallas kernels, all_shares(): pl.pallas_call(share_kernel, grid=(wide // tile,), in_specs=[pl.BlockSpec...  7.24 us
    unnamed x91, local copies, waits for them, and re-layouts  6.47 us
    pallas_call x1, Pallas kernels, add_table(): pl.pallas_call(add_table_kernel, grid=(rows // tile,), in_specs=[pl.Block...  5.3 us
  transfers between devices with their start and end apart: 35, of which 18 were waited for; matrix products, arithmetic and copies ran while one was open for 25% of the time, Pallas kernels for 3%

profile of v2, /device:TPU:33, one launch (start us, length us, event | category | flops | bytes accessed | tf_op | source)
XLA Modules:
  0.0 257.9 jit_solution(14076330131074918556)
XLA Ops:
  2.7 5.3 %shard_map.93 = bf16[128,768]{1,0:T(8,128)(2,1)} custom-call(f32[128,1]{1,0:T(8,128)} %copy.13.place_ref, f32[1,768]{1,0:T(1,128)} %negate_power_fusion.freq_ref, bf16[128,768]{1,0:T(8,128)(2,1)} %normed_ref.1), custom_call_target="tpu_custom_call" | custom-call | tf_op jit(solution)/shard_map/pallas_call | solution.py:26
  11.5 5.2 %collective-permute-start.1 = (bf16[64,1536]{1,0:T(8,128)(2,1)S(1)}, bf16[64,1536]{1,0:T(8,128)(2,1)S(1)}, u32[]{:S(2)}, u32[]{:S(2)}) collective-permute-start(bf16[64,1536]{1,0:T(8,128)(2,1)S(1)} %pad_maximum_fusion.15), channel_id=1, source_target_pairs={{0,12},{1,13},{2,14},{3,15},{4,0},{5,1},{6,2},{7,3},{8,4},{9,5},{1... | collective-permute-start | bytes 589832 | tf_op jit(solution)/shard_map/ppermute | solution.py:73
  20.9 4.2 %all-to-all-start = ((bf16[4,64,1536]{2,1,0:T(8,128)(2,1)}), bf16[4,64,1536]{2,1,0:T(8,128)(2,1)S(1)}, u32[]{:S(2)}, u32[]{:S(2)}) async-start(bf16[4,64,1536]{2,1,0:T(8,128)(2,1)} %broadcast_in_dim.11), calls=%async_computation | async-start | bytes 1572864 | tf_op jit(solution)/shard_map/all_to_all | solution.py:141
  29.1 6.5 %collective-permute-done.2 = bf16[64,1536]{1,0:T(8,128)(2,1)S(1)} collective-permute-done((bf16[64,1536]{1,0:T(8,128)(2,1)S(1)}, bf16[64,1536]{1,0:T(8,128)(2,1)S(1)}, u32[]{:S(2)}, u32[]{:S(2)}) %collective-permute-start.2) | collective-permute-done | bytes 196640 | tf_op jit(solution)/shard_map/ppermute | solution.py:73
  46.1 9.8 %collective-permute-done.8 = bf16[256,1536]{1,0:T(8,128)(2,1)S(1)} collective-permute-done((bf16[256,1536]{1,0:T(8,128)(2,1)S(1)}, bf16[256,1536]{1,0:T(8,128)(2,1)S(1)}, u32[]{:S(2)}, u32[]{:S(2)}) %collective-permute-start.8) | collective-permute-done | bytes 786464 | tf_op jit(solution)/shard_map/ppermute | solution.py:73
  55.9 3.2 %collective-permute-done.9 = bf16[256,1536]{1,0:T(8,128)(2,1)} collective-permute-done((bf16[256,1536]{1,0:T(8,128)(2,1)S(1)}, bf16[256,1536]{1,0:T(8,128)(2,1)}, u32[]{:S(2)}, u32[]{:S(2)}) %collective-permute-start.9) | collective-permute-done | bytes 786464 | tf_op jit(solution)/shard_map/ppermute | solution.py:73
  62.8 3.8 %collective-permute-start.6 = (bf16[4,64,1536]{2,1,0:T(8,128)(2,1)S(1)}, bf16[4,64,1536]{2,1,0:T(8,128)(2,1)}, u32[]{:S(2)}, u32[]{:S(2)}) collective-permute-start(bf16[4,64,1536]{2,1,0:T(8,128)(2,1)S(1)} %fusion.14), channel_id=1, source_target_pairs={{0,12},{1,13},{2,14},{3,15},{4,0},{5,1},{6,2},{7,3},{8,4},{9,5},{1... | collective-permute-start | bytes 2359304 | tf_op jit(solution)/shard_map/ppermute | solution.py:73
  67.8 4.0 %all-to-all-start.1 = ((bf16[4,3,64,768]{3,2,1,0:T(8,128)(2,1)}), bf16[4,3,64,768]{3,2,1,0:T(8,128)(2,1)S(1)}, u32[]{:S(2)}, u32[]{:S(2)}) async-start(bf16[4,3,64,768]{3,2,1,0:T(8,128)(2,1)} %pad_maximum_fusion.3), calls=%async_computation.1 | async-start | bytes 2359296 | tf_op jit(solution)/shard_map/all_to_all | solution.py:120
  85.9 3.5 %all-to-all-start.2 = ((bf16[4,1,64,768]{3,2,1,0:T(8,128)(2,1)}), bf16[4,1,64,768]{3,2,1,0:T(8,128)(2,1)S(1)}, u32[]{:S(2)}, u32[]{:S(2)}) async-start(bf16[4,1,64,768]{3,2,1,0:T(8,128)(2,1)} %bitcast.22), calls=%async_computation.2 | async-start | bytes 786432 | tf_op jit(solution)/shard_map/all_to_all | solution.py:120
  89.4 3.2 %convolution_convert_fusion.11 = bf16[256,768]{1,0:T(8,128)(2,1)} fusion(bf16[256,1536]{1,0:T(8,128)(2,1)S(1)} %bitcast.56, bf16[768,1536]{1,0:T(8,128)(2,1)} %copy-done.23), kind=kOutput, calls=%fused_computation.26 | convolution fusion | flops 604176384 | bytes 3538944 | tf_op jit(solution)/shard_map/dot_general | solution.py:77
  92.7 7.0 %collective-permute-done.6 = bf16[4,64,1536]{2,1,0:T(8,128)(2,1)} collective-permute-done((bf16[4,64,1536]{2,1,0:T(8,128)(2,1)S(1)}, bf16[4,64,1536]{2,1,0:T(8,128)(2,1)}, u32[]{:S(2)}, u32[]{:S(2)}) %collective-permute-start.6) | collective-permute-done | bytes 786464 | tf_op jit(solution)/shard_map/ppermute | solution.py:73
  108.6 4.0 %all-to-all-start.3 = ((bf16[4,4,64,768]{3,2,1,0:T(8,128)(2,1)}), bf16[4,4,64,768]{3,2,1,0:T(8,128)(2,1)S(1)}, u32[]{:S(2)}, u32[]{:S(2)}) async-start(bf16[4,4,64,768]{3,2,1,0:T(8,128)(2,1)} %broadcast_in_dim.13), calls=%async_computation.3 | async-start | bytes 3145728 | tf_op jit(solution)/shard_map/all_to_all | solution.py:120
  121.0 11.0 %all-to-all-done.3 = bf16[4,4,64,768]{3,2,1,0:T(8,128)(2,1)S(1)} async-done(((bf16[4,4,64,768]{3,2,1,0:T(8,128)(2,1)}), bf16[4,4,64,768]{3,2,1,0:T(8,128)(2,1)S(1)}, u32[]{:S(2)}, u32[]{:S(2)}) %all-to-all-start.3) | async-done | bytes 1572896 | tf_op jit(solution)/shard_map/all_to_all | solution.py:120
  133.1 3.6 %all-to-all-start.4 = ((bf16[4,4,64,768]{3,2,1,0:T(8,128)(2,1)}), bf16[4,4,64,768]{3,2,1,0:T(8,128)(2,1)S(1)}, u32[]{:S(2)}, u32[]{:S(2)}) async-start(bf16[4,4,64,768]{3,2,1,0:T(8,128)(2,1)} %pad_maximum_fusion), calls=%async_computation.4 | async-start | bytes 3145728 | tf_op jit(solution)/shard_map/all_to_all | solution.py:120
  146.7 8.4 %all-to-all-done.4 = bf16[4,4,64,768]{3,2,1,0:T(8,128)(2,1)S(1)} async-done(((bf16[4,4,64,768]{3,2,1,0:T(8,128)(2,1)}), bf16[4,4,64,768]{3,2,1,0:T(8,128)(2,1)S(1)}, u32[]{:S(2)}, u32[]{:S(2)}) %all-to-all-start.4) | async-done | bytes 1572896 | tf_op jit(solution)/shard_map/all_to_all | solution.py:120
  157.2 3.7 %all-to-all-start.5 = ((bf16[4,4,64,768]{3,2,1,0:T(8,128)(2,1)}), bf16[4,4,64,768]{3,2,1,0:T(8,128)(2,1)S(1)}, u32[]{:S(2)}, u32[]{:S(2)}) async-start(bf16[4,4,64,768]{3,2,1,0:T(8,128)(2,1)} %broadcast_in_dim.14), calls=%async_computation.5 | async-start | bytes 3145728 | tf_op jit(solution)/shard_map/all_to_all | solution.py:120
  169.1 9.3 %all-to-all-done.5.d_ref = bf16[4,4,64,768]{3,2,1,0:T(8,128)(2,1)S(1)} async-done(((bf16[4,4,64,768]{3,2,1,0:T(8,128)(2,1)}), bf16[4,4,64,768]{3,2,1,0:T(8,128)(2,1)S(1)}, u32[]{:S(2)}, u32[]{:S(2)}) %all-to-all-start.5) | async-done | bytes 1572896 | tf_op jit(solution)/shard_map/all_to_all | solution.py:120
  179.5 7.2 %shard_map.94 = (bf16[256,1536]{1,0:T(8,128)(2,1)}, bf16[256,1536]{1,0:T(8,128)(2,1)}, bf16[256,1536]{1,0:T(8,128)(2,1)}, f32[256,1536]{1,0:T(8,128)}) custom-call(bf16[4,4,64,768]{3,2,1,0:T(8,128)(2,1)} %copy-done, bf16[1536,768]{1,0:T(8,128)(2,1)} %constant_dynamic-update-slice_fusion.2.w_ref), custom_call_target="tpu_custom_call" | custom-call | flops 2415919104 | bytes 7864320 | tf_op jit(solution)/shard_map/pallas_call | solution.py:93
  190.0 4.2 %collective-permute-start.20 = (bf16[400,768]{1,0:T(8,128)(2,1)}, bf16[400,768]{1,0:T(8,128)(2,1)}, u32[]{:S(2)}, u32[]{:S(2)}) collective-permute-start(bf16[400,768]{1,0:T(8,128)(2,1)} %convolution_convert_fusion), channel_id=1, source_target_pairs={{0,16},{1,17},{2,18},{3,19},{4,20},{5,21},{6,22},{7,23},{8,24},{9,... | collective-permute-start | bytes 1843208 | tf_op jit(solution)/shard_map/ppermute | solution.py:73
  205.1 11.1 %collective-permute-done.14 = bf16[256,1536]{1,0:T(8,128)(2,1)S(1)} collective-permute-done((bf16[256,1536]{1,0:T(8,128)(2,1)}, bf16[256,1536]{1,0:T(8,128)(2,1)S(1)}, u32[]{:S(2)}, u32[]{:S(2)}) %collective-permute-start.14) | collective-permute-done | bytes 786464 | tf_op jit(solution)/shard_map/ppermute | solution.py:73
  216.3 17.2 %collective-permute-done.15 = bf16[256,1536]{1,0:T(8,128)(2,1)S(1)} collective-permute-done((bf16[256,1536]{1,0:T(8,128)(2,1)}, bf16[256,1536]{1,0:T(8,128)(2,1)S(1)}, u32[]{:S(2)}, u32[]{:S(2)}) %collective-permute-start.15) | collective-permute-done | bytes 786464 | tf_op jit(solution)/shard_map/ppermute | solution.py:73
  239.6 3.1 %convert_add_fusion = f32[768,768]{1,0:T(8,128)} fusion(bf16[384,768]{1,0:T(8,128)(2,1)S(1)} %add_convert_fusion.2, bf16[384,768]{1,0:T(8,128)(2,1)} %add_convert_fusion.3, bf16[384,768]{1,0:T(8,128)(2,1)} %collective-permute-done.28, bf16[384,768]{1,0:T(8,128)(2,1)} %collective-permute-done.27), kind=kLoop, calls=%fused_computation.1 | loop fusion | flops 5308416 | bytes 4718592 | tf_op jit(solution)/shard_map/add | solution.py:198
  242.6 3.7 %collective-permute-done.21 = bf16[64,1536]{1,0:T(8,128)(2,1)S(1)} collective-permute-done((bf16[64,1536]{1,0:T(8,128)(2,1)S(1)}, bf16[64,1536]{1,0:T(8,128)(2,1)S(1)}, u32[]{:S(2)}, u32[]{:S(2)}) %collective-permute-start.21) | collective-permute-done | bytes 196640 | tf_op jit(solution)/shard_map/ppermute | solution.py:73
  248.6 5.1 %collective-permute-done.23 = bf16[64,1536]{1,0:T(8,128)(2,1)S(1)} collective-permute-done((bf16[64,1536]{1,0:T(8,128)(2,1)S(1)}, bf16[64,1536]{1,0:T(8,128)(2,1)S(1)}, u32[]{:S(2)}, u32[]{:S(2)}) %collective-permute-start.23) | collective-permute-done | bytes 196640 | tf_op jit(solution)/shard_map/ppermute | solution.py:73
  (206 shorter events, 109.1 us)
Async XLA Ops:
  9.8 31.2 %collective-permute-start.4 = (bf16[768,768]{1,0:T(8,128)(2,1)}, bf16[768,768]{1,0:T(8,128)(2,1)}, u32[]{:S(2)}, u32[]{:S(2)}) collective-permute-start(bf16[768,768]{1,0:T(8,128)(2,1)} %param.9), channel_id=1, source_target_pairs={{0,16},{1,17},{2,18},{3,19},{4,20},{5,21},{6,22},{7,23},{8,24},{9,... | collective-permute-start | bytes 3538952 | tf_op jit(solution)/shard_map/ppermute | solution.py:73
  9.9 52.9 %collective-permute-start.5 = (bf16[768,768]{1,0:T(8,128)(2,1)}, bf16[768,768]{1,0:T(8,128)(2,1)}, u32[]{:S(2)}, u32[]{:S(2)}) collective-permute-start(bf16[768,768]{1,0:T(8,128)(2,1)} %param.11), channel_id=1, source_target_pairs={{0,16},{1,17},{2,18},{3,19},{4,20},{5,21},{6,22},{7,23},{8,24},{9,... | collective-permute-start | bytes 3538952 | tf_op jit(solution)/shard_map/ppermute | solution.py:73
  11.5 17.6 %collective-permute-start.1 = (bf16[64,1536]{1,0:T(8,128)(2,1)S(1)}, bf16[64,1536]{1,0:T(8,128)(2,1)S(1)}, u32[]{:S(2)}, u32[]{:S(2)}) collective-permute-start(bf16[64,1536]{1,0:T(8,128)(2,1)S(1)} %pad_maximum_fusion.15), channel_id=1, source_target_pairs={{0,12},{1,13},{2,14},{3,15},{4,0},{5,1},{6,2},{7,3},{8,4},{9,5},{1... | collective-permute-start | bytes 589832 | tf_op jit(solution)/shard_map/ppermute | solution.py:73
  16.7 18.8 %collective-permute-start.2 = (bf16[64,1536]{1,0:T(8,128)(2,1)S(1)}, bf16[64,1536]{1,0:T(8,128)(2,1)S(1)}, u32[]{:S(2)}, u32[]{:S(2)}) collective-permute-start(bf16[64,1536]{1,0:T(8,128)(2,1)S(1)} %pad_maximum_fusion.15), channel_id=1, source_target_pairs={{0,8},{1,9},{2,10},{3,11},{4,12},{5,13},{6,14},{7,15},{8,0},{9,1},... | collective-permute-start | bytes 589832 | tf_op jit(solution)/shard_map/ppermute | solution.py:73
  17.9 18.5 %collective-permute-start.3 = (bf16[64,1536]{1,0:T(8,128)(2,1)S(1)}, bf16[64,1536]{1,0:T(8,128)(2,1)S(1)}, u32[]{:S(2)}, u32[]{:S(2)}) collective-permute-start(bf16[64,1536]{1,0:T(8,128)(2,1)S(1)} %pad_maximum_fusion.15), channel_id=1, source_target_pairs={{0,4},{1,5},{2,6},{3,7},{4,8},{5,9},{6,10},{7,11},{8,12},{9,13},{1... | collective-permute-start | bytes 589832 | tf_op jit(solution)/shard_map/ppermute | solution.py:73
  20.9 19.7 %all-to-all-start = ((bf16[4,64,1536]{2,1,0:T(8,128)(2,1)}), bf16[4,64,1536]{2,1,0:T(8,128)(2,1)S(1)}, u32[]{:S(2)}, u32[]{:S(2)}) async-start(bf16[4,64,1536]{2,1,0:T(8,128)(2,1)} %broadcast_in_dim.11), calls=%async_computation | async-start | bytes 1572864 | tf_op jit(solution)/shard_map/all_to_all | solution.py:141
  37.1 18.8 %collective-permute-start.8 = (bf16[256,1536]{1,0:T(8,128)(2,1)S(1)}, bf16[256,1536]{1,0:T(8,128)(2,1)S(1)}, u32[]{:S(2)}, u32[]{:S(2)}) collective-permute-start(bf16[256,1536]{1,0:T(8,128)(2,1)S(1)} %pad_maximum_fusion.4), channel_id=1, source_target_pairs={{0,3},{1,0},{2,1},{3,2},{4,7},{5,4},{6,5},{7,6},{8,11},{9,8},{10,9... | collective-permute-start | bytes 2359304 | tf_op jit(solution)/shard_map/ppermute | solution.py:73
  39.7 19.4 %collective-permute-start.9 = (bf16[256,1536]{1,0:T(8,128)(2,1)S(1)}, bf16[256,1536]{1,0:T(8,128)(2,1)}, u32[]{:S(2)}, u32[]{:S(2)}) collective-permute-start(bf16[256,1536]{1,0:T(8,128)(2,1)S(1)} %pad_maximum_fusion.4), channel_id=1, source_target_pairs={{0,1},{1,2},{2,3},{3,0},{4,5},{5,6},{6,7},{7,4},{8,9},{9,10},{10,1... | collective-permute-start | bytes 2359304 | tf_op jit(solution)/shard_map/ppermute | solution.py:73
  62.8 36.8 %collective-permute-start.6 = (bf16[4,64,1536]{2,1,0:T(8,128)(2,1)S(1)}, bf16[4,64,1536]{2,1,0:T(8,128)(2,1)}, u32[]{:S(2)}, u32[]{:S(2)}) collective-permute-start(bf16[4,64,1536]{2,1,0:T(8,128)(2,1)S(1)} %fusion.14), channel_id=1, source_target_pairs={{0,12},{1,13},{2,14},{3,15},{4,0},{5,1},{6,2},{7,3},{8,4},{9,5},{1... | collective-permute-start | bytes 2359304 | tf_op jit(solution)/shard_map/ppermute | solution.py:73
  66.6 35.7 %collective-permute-start.7 = (bf16[4,64,1536]{2,1,0:T(8,128)(2,1)S(1)}, bf16[4,64,1536]{2,1,0:T(8,128)(2,1)}, u32[]{:S(2)}, u32[]{:S(2)}) collective-permute-start(bf16[4,64,1536]{2,1,0:T(8,128)(2,1)S(1)} %fusion.14), channel_id=1, source_target_pairs={{0,4},{1,5},{2,6},{3,7},{4,8},{5,9},{6,10},{7,11},{8,12},{9,13},{1... | collective-permute-start | bytes 2359304 | tf_op jit(solution)/shard_map/ppermute | solution.py:73
  67.8 18.0 %all-to-all-start.1 = ((bf16[4,3,64,768]{3,2,1,0:T(8,128)(2,1)}), bf16[4,3,64,768]{3,2,1,0:T(8,128)(2,1)S(1)}, u32[]{:S(2)}, u32[]{:S(2)}) async-start(bf16[4,3,64,768]{3,2,1,0:T(8,128)(2,1)} %pad_maximum_fusion.3), calls=%async_computation.1 | async-start | bytes 2359296 | tf_op jit(solution)/shard_map/all_to_all | solution.py:120
  85.9 21.0 %all-to-all-start.2 = ((bf16[4,1,64,768]{3,2,1,0:T(8,128)(2,1)}), bf16[4,1,64,768]{3,2,1,0:T(8,128)(2,1)S(1)}, u32[]{:S(2)}, u32[]{:S(2)}) async-start(bf16[4,1,64,768]{3,2,1,0:T(8,128)(2,1)} %bitcast.22), calls=%async_computation.2 | async-start | bytes 786432 | tf_op jit(solution)/shard_map/all_to_all | solution.py:120
  108.6 23.4 %all-to-all-start.3 = ((bf16[4,4,64,768]{3,2,1,0:T(8,128)(2,1)}), bf16[4,4,64,768]{3,2,1,0:T(8,128)(2,1)S(1)}, u32[]{:S(2)}, u32[]{:S(2)}) async-start(bf16[4,4,64,768]{3,2,1,0:T(8,128)(2,1)} %broadcast_in_dim.13), calls=%async_computation.3 | async-start | bytes 3145728 | tf_op jit(solution)/shard_map/all_to_all | solution.py:120
  133.1 22.0 %all-to-all-start.4 = ((bf16[4,4,64,768]{3,2,1,0:T(8,128)(2,1)}), bf16[4,4,64,768]{3,2,1,0:T(8,128)(2,1)S(1)}, u32[]{:S(2)}, u32[]{:S(2)}) async-start(bf16[4,4,64,768]{3,2,1,0:T(8,128)(2,1)} %pad_maximum_fusion), calls=%async_computation.4 | async-start | bytes 3145728 | tf_op jit(solution)/shard_map/all_to_all | solution.py:120
  142.7 19.2 %collective-permute-start.18 = (bf16[384,768]{1,0:T(8,128)(2,1)}, bf16[384,768]{1,0:T(8,128)(2,1)}, u32[]{:S(2)}, u32[]{:S(2)}) collective-permute-start(bf16[384,768]{1,0:T(8,128)(2,1)} %convolution_convert_fusion.2), channel_id=1, source_target_pairs={{0,16},{1,17},{2,18},{3,19},{4,20},{5,21},{6,22},{7,23},{8,24},{9,... | collective-permute-start | bytes 1769480 | tf_op jit(solution)/shard_map/ppermute | solution.py:73
  146.7 18.2 %collective-permute-start.17 = (bf16[384,768]{1,0:T(8,128)(2,1)}, bf16[384,768]{1,0:T(8,128)(2,1)}, u32[]{:S(2)}, u32[]{:S(2)}) collective-permute-start(bf16[384,768]{1,0:T(8,128)(2,1)} %convolution_convert_fusion.3), channel_id=1, source_target_pairs={{0,16},{1,17},{2,18},{3,19},{4,20},{5,21},{6,22},{7,23},{8,24},{9,... | collective-permute-start | bytes 1769480 | tf_op jit(solution)/shard_map/ppermute | solution.py:73
  157.2 21.2 %all-to-all-start.5 = ((bf16[4,4,64,768]{3,2,1,0:T(8,128)(2,1)}), bf16[4,4,64,768]{3,2,1,0:T(8,128)(2,1)S(1)}, u32[]{:S(2)}, u32[]{:S(2)}) async-start(bf16[4,4,64,768]{3,2,1,0:T(8,128)(2,1)} %broadcast_in_dim.14), calls=%async_computation.5 | async-start | bytes 3145728 | tf_op jit(solution)/shard_map/all_to_all | solution.py:120
  164.8 31.1 %collective-permute-start.28 = (bf16[384,768]{1,0:T(8,128)(2,1)S(1)}, bf16[384,768]{1,0:T(8,128)(2,1)}, u32[]{:S(2)}, u32[]{:S(2)}) collective-permute-start(bf16[384,768]{1,0:T(8,128)(2,1)S(1)} %add_convert_fusion.2), channel_id=1, source_target_pairs={{0,128},{1,129},{2,130},{3,131},{4,132},{5,133},{6,134},{7,135},{8... | collective-permute-start | bytes 1769480 | tf_op jit(solution)/shard_map/ppermute | solution.py:73
  167.6 29.1 %collective-permute-start.27 = (bf16[384,768]{1,0:T(8,128)(2,1)}, bf16[384,768]{1,0:T(8,128)(2,1)}, u32[]{:S(2)}, u32[]{:S(2)}) collective-permute-start(bf16[384,768]{1,0:T(8,128)(2,1)} %add_convert_fusion.3), channel_id=1, source_target_pairs={{0,128},{1,129},{2,130},{3,131},{4,132},{5,133},{6,134},{7,135},{8... | collective-permute-start | bytes 1769480 | tf_op jit(solution)/shard_map/ppermute | solution.py:73
  195.9 20.4 %collective-permute-start.14 = (bf16[256,1536]{1,0:T(8,128)(2,1)}, bf16[256,1536]{1,0:T(8,128)(2,1)S(1)}, u32[]{:S(2)}, u32[]{:S(2)}) collective-permute-start(bf16[256,1536]{1,0:T(8,128)(2,1)} %get-tuple-element.48), channel_id=1, source_target_pairs={{0,2},{1,3},{2,0},{3,1},{4,6},{5,7},{6,4},{7,5},{8,10},{9,11},{10,... | collective-permute-start | bytes 2359304 | tf_op jit(solution)/shard_map/ppermute | solution.py:73
  195.9 37.6 %collective-permute-start.15 = (bf16[256,1536]{1,0:T(8,128)(2,1)}, bf16[256,1536]{1,0:T(8,128)(2,1)S(1)}, u32[]{:S(2)}, u32[]{:S(2)}) collective-permute-start(bf16[256,1536]{1,0:T(8,128)(2,1)} %get-tuple-element.49), channel_id=1, source_target_pairs={{0,1},{1,2},{2,3},{3,0},{4,5},{5,6},{6,7},{7,4},{8,9},{9,10},{10,1... | collective-permute-start | bytes 2359304 | tf_op jit(solution)/shard_map/ppermute | solution.py:73
  196.7 36.7 %collective-permute-start.16 = (bf16[256,1536]{1,0:T(8,128)(2,1)}, bf16[256,1536]{1,0:T(8,128)(2,1)S(1)}, u32[]{:S(2)}, u32[]{:S(2)}) collective-permute-start(bf16[256,1536]{1,0:T(8,128)(2,1)} %get-tuple-element.50), channel_id=1, source_target_pairs={{0,3},{1,0},{2,1},{3,2},{4,7},{5,4},{6,5},{7,6},{8,11},{9,8},{10,9... | collective-permute-start | bytes 2359304 | tf_op jit(solution)/shard_map/ppermute | solution.py:73
  201.5 52.2 %collective-permute-start.25 = (bf16[400,768]{1,0:T(8,128)(2,1)S(1)}, bf16[400,768]{1,0:T(8,128)(2,1)S(1)}, u32[]{:S(2)}, u32[]{:S(2)}) collective-permute-start(bf16[400,768]{1,0:T(8,128)(2,1)S(1)} %pad_maximum_fusion.9), channel_id=1, source_target_pairs={{0,128},{1,129},{2,130},{3,131},{4,132},{5,133},{6,134},{7,135},{8... | collective-permute-start | bytes 1843208 | tf_op jit(solution)/shard_map/ppermute | solution.py:73
  203.6 50.1 %collective-permute-start.24 = (bf16[384,768]{1,0:T(8,128)(2,1)S(1)}, bf16[384,768]{1,0:T(8,128)(2,1)S(1)}, u32[]{:S(2)}, u32[]{:S(2)}) collective-permute-start(bf16[384,768]{1,0:T(8,128)(2,1)S(1)} %add_convert_fusion.1), channel_id=1, source_target_pairs={{0,128},{1,129},{2,130},{3,131},{4,132},{5,133},{6,134},{7,135},{8... | collective-permute-start | bytes 1769480 | tf_op jit(solution)/shard_map/ppermute | solution.py:73
  (55 other events, 367.8 us)

commit v3 on v1

--- a/solution.py
+++ b/solution.py
@@ -89,7 +89,7 @@
 
 def all_shares(d_pre, w):
     rows, wide, hidden = 4 * d_pre.shape[2], w.shape[0], w.shape[1]
-    tile = 256
+    tile = 512
     return pl.pallas_call(
         share_kernel,
         grid=(wide // tile,),

time: 246 us -> 246 us (level)
  no operation moved by 1% of the time
where the time goes in v3:
time: 246 us; the launch traced here: 244 us
  waiting for transfers between devices  79.6 us (32%)
  starting transfers between devices  75.1 us (31%)
  matrix products  30.5 us (12%)
  local copies, waits for them, and re-layouts  29.3 us (12%)
  other arithmetic  16.3 us (7%)
  Pallas kernels  11.6 us (5%)
    ppermute x29, waiting for transfers between devices, send(): return lax.ppermute(value, AXES, pairs)  61.6 us
    ppermute x29, starting transfers between devices, send(): return lax.ppermute(value, AXES, pairs)  51.6 us
    dot_general x16, matrix products, dot(): lax.dot_general(a, b, ((contract[:1], contract[1:]), ((), ())), preferred...  30.5 us
    all_to_all x5, starting transfers between devices, swap_x(): lax.all_to_all(value, 'row', 0, 0, tiled=True, axis_index_groups=X_SETS)  19.3 us
    all_to_all x5, waiting for transfers between devices, swap_x(): lax.all_to_all(value, 'row', 0, 0, tiled=True, axis_index_groups=X_SETS)  18 us
    unnamed x93, local copies, waits for them, and re-layouts  7.41 us
    pallas_call x1, Pallas kernels, all_shares(): pl.pallas_call(share_kernel, grid=(wide // tile,), in_specs=[pl.BlockSpec...  6.32 us
    pallas_call x1, Pallas kernels, add_table(): pl.pallas_call(add_table_kernel, grid=(rows // tile,), in_specs=[pl.Block...  5.3 us
  transfers between devices with their start and end apart: 35, of which 15 were waited for; matrix products, arithmetic and copies ran while one was open for 28% of the time, Pallas kernels for 3%

profile of v3, /device:TPU:1, one launch (start us, length us, event | category | flops | bytes accessed | tf_op | source)
XLA Modules:
  0.0 243.7 jit_solution(7759449491747216931)
XLA Ops:
  2.8 5.3 %shard_map.93 = bf16[128,768]{1,0:T(8,128)(2,1)} custom-call(f32[128,1]{1,0:T(8,128)} %copy.13.place_ref, f32[1,768]{1,0:T(1,128)} %negate_power_fusion.freq_ref, bf16[128,768]{1,0:T(8,128)(2,1)} %normed_ref.1), custom_call_target="tpu_custom_call" | custom-call | tf_op jit(solution)/shard_map/pallas_call | solution.py:26
  9.1 3.3 %collective-permute-start = (bf16[2,64,768]{2,1,0:T(8,128)(2,1)S(1)}, bf16[2,64,768]{2,1,0:T(8,128)(2,1)S(1)}, u32[]{:S(2)}, u32[]{:S(2)}) collective-permute-start(bf16[2,64,768]{2,1,0:T(8,128)(2,1)S(1)} %get-tuple-element.98), channel_id=1, source_target_pairs={{0,16},{1,17},{2,18},{3,19},{4,20},{5,21},{6,22},{7,23},{8,24},{9,... | collective-permute-start | bytes 589832 | tf_op jit(solution)/shard_map/ppermute | solution.py:73
  15.5 5.1 %collective-permute-start.2 = (bf16[64,1536]{1,0:T(8,128)(2,1)S(1)}, bf16[64,1536]{1,0:T(8,128)(2,1)S(1)}, u32[]{:S(2)}, u32[]{:S(2)}) collective-permute-start(bf16[64,1536]{1,0:T(8,128)(2,1)S(1)} %pad_maximum_fusion.15), channel_id=1, source_target_pairs={{0,8},{1,9},{2,10},{3,11},{4,12},{5,13},{6,14},{7,15},{8,0},{9,1},... | collective-permute-start | bytes 589832 | tf_op jit(solution)/shard_map/ppermute | solution.py:73
  24.0 4.2 %all-to-all-start = ((bf16[4,64,1536]{2,1,0:T(8,128)(2,1)}), bf16[4,64,1536]{2,1,0:T(8,128)(2,1)S(1)}, u32[]{:S(2)}, u32[]{:S(2)}) async-start(bf16[4,64,1536]{2,1,0:T(8,128)(2,1)} %broadcast_in_dim.11), calls=%async_computation | async-start | bytes 1572864 | tf_op jit(solution)/shard_map/all_to_all | solution.py:141
  29.2 3.5 %collective-permute-done.2 = bf16[64,1536]{1,0:T(8,128)(2,1)S(1)} collective-permute-done((bf16[64,1536]{1,0:T(8,128)(2,1)S(1)}, bf16[64,1536]{1,0:T(8,128)(2,1)S(1)}, u32[]{:S(2)}, u32[]{:S(2)}) %collective-permute-start.2) | collective-permute-done | bytes 196640 | tf_op jit(solution)/shard_map/ppermute | solution.py:73
  32.8 6.5 %collective-permute-done.1 = bf16[64,1536]{1,0:T(8,128)(2,1)S(1)} collective-permute-done((bf16[64,1536]{1,0:T(8,128)(2,1)S(1)}, bf16[64,1536]{1,0:T(8,128)(2,1)S(1)}, u32[]{:S(2)}, u32[]{:S(2)}) %collective-permute-start.1) | collective-permute-done | bytes 196640 | tf_op jit(solution)/shard_map/ppermute | solution.py:73
  44.1 3.4 %collective-permute-start.6 = (bf16[4,64,1536]{2,1,0:T(8,128)(2,1)S(1)}, bf16[4,64,1536]{2,1,0:T(8,128)(2,1)}, u32[]{:S(2)}, u32[]{:S(2)}) collective-permute-start(bf16[4,64,1536]{2,1,0:T(8,128)(2,1)S(1)} %fusion.14), channel_id=1, source_target_pairs={{0,12},{1,13},{2,14},{3,15},{4,0},{5,1},{6,2},{7,3},{8,4},{9,5},{1... | collective-permute-start | bytes 2359304 | tf_op jit(solution)/shard_map/ppermute | solution.py:73
  52.4 6.8 %collective-permute-done.8 = bf16[256,1536]{1,0:T(8,128)(2,1)S(1)} collective-permute-done((bf16[256,1536]{1,0:T(8,128)(2,1)S(1)}, bf16[256,1536]{1,0:T(8,128)(2,1)S(1)}, u32[]{:S(2)}, u32[]{:S(2)}) %collective-permute-start.8) | collective-permute-done | bytes 786464 | tf_op jit(solution)/shard_map/ppermute | solution.py:73
  69.6 4.0 %all-to-all-start.1 = ((bf16[4,3,64,768]{3,2,1,0:T(8,128)(2,1)}), bf16[4,3,64,768]{3,2,1,0:T(8,128)(2,1)S(1)}, u32[]{:S(2)}, u32[]{:S(2)}) async-start(bf16[4,3,64,768]{3,2,1,0:T(8,128)(2,1)} %pad_maximum_fusion.3), calls=%async_computation.1 | async-start | bytes 2359296 | tf_op jit(solution)/shard_map/all_to_all | solution.py:120
  81.6 6.0 %all-to-all-done.1 = bf16[4,3,64,768]{3,2,1,0:T(8,128)(2,1)S(1)} async-done(((bf16[4,3,64,768]{3,2,1,0:T(8,128)(2,1)}), bf16[4,3,64,768]{3,2,1,0:T(8,128)(2,1)S(1)}, u32[]{:S(2)}, u32[]{:S(2)}) %all-to-all-start.1) | async-done | bytes 1179680 | tf_op jit(solution)/shard_map/all_to_all | solution.py:120
  87.8 3.5 %all-to-all-start.2 = ((bf16[4,1,64,768]{3,2,1,0:T(8,128)(2,1)}), bf16[4,1,64,768]{3,2,1,0:T(8,128)(2,1)S(1)}, u32[]{:S(2)}, u32[]{:S(2)}) async-start(bf16[4,1,64,768]{3,2,1,0:T(8,128)(2,1)} %bitcast.22), calls=%async_computation.2 | async-start | bytes 786432 | tf_op jit(solution)/shard_map/all_to_all | solution.py:120
  102.1 4.2 %all-to-all-start.3 = ((bf16[4,4,64,768]{3,2,1,0:T(8,128)(2,1)}), bf16[4,4,64,768]{3,2,1,0:T(8,128)(2,1)S(1)}, u32[]{:S(2)}, u32[]{:S(2)}) async-start(bf16[4,4,64,768]{3,2,1,0:T(8,128)(2,1)} %broadcast_in_dim.13), calls=%async_computation.3 | async-start | bytes 3145728 | tf_op jit(solution)/shard_map/all_to_all | solution.py:120
  116.4 5.7 %all-to-all-done.3 = bf16[4,4,64,768]{3,2,1,0:T(8,128)(2,1)S(1)} async-done(((bf16[4,4,64,768]{3,2,1,0:T(8,128)(2,1)}), bf16[4,4,64,768]{3,2,1,0:T(8,128)(2,1)S(1)}, u32[]{:S(2)}, u32[]{:S(2)}) %all-to-all-start.3) | async-done | bytes 1572896 | tf_op jit(solution)/shard_map/all_to_all | solution.py:120
  123.3 3.6 %all-to-all-start.4 = ((bf16[4,4,64,768]{3,2,1,0:T(8,128)(2,1)}), bf16[4,4,64,768]{3,2,1,0:T(8,128)(2,1)S(1)}, u32[]{:S(2)}, u32[]{:S(2)}) async-start(bf16[4,4,64,768]{3,2,1,0:T(8,128)(2,1)} %pad_maximum_fusion), calls=%async_computation.4 | async-start | bytes 3145728 | tf_op jit(solution)/shard_map/all_to_all | solution.py:120
  132.8 5.8 %collective-permute-start.14 = (bf16[384,768]{1,0:T(8,128)(2,1)}, bf16[384,768]{1,0:T(8,128)(2,1)}, u32[]{:S(2)}, u32[]{:S(2)}) collective-permute-start(bf16[384,768]{1,0:T(8,128)(2,1)} %convolution_convert_fusion.3), channel_id=1, source_target_pairs={{0,16},{1,17},{2,18},{3,19},{4,20},{5,21},{6,22},{7,23},{8,24},{9,... | collective-permute-start | bytes 1769480 | tf_op jit(solution)/shard_map/ppermute | solution.py:73
  143.6 4.0 %all-to-all-start.5 = ((bf16[4,4,64,768]{3,2,1,0:T(8,128)(2,1)}), bf16[4,4,64,768]{3,2,1,0:T(8,128)(2,1)S(1)}, u32[]{:S(2)}, u32[]{:S(2)}) async-start(bf16[4,4,64,768]{3,2,1,0:T(8,128)(2,1)} %broadcast_in_dim.14), calls=%async_computation.5 | async-start | bytes 3145728 | tf_op jit(solution)/shard_map/all_to_all | solution.py:120
  156.6 4.9 %all-to-all-done.5.d_ref = bf16[4,4,64,768]{3,2,1,0:T(8,128)(2,1)S(1)} async-done(((bf16[4,4,64,768]{3,2,1,0:T(8,128)(2,1)}), bf16[4,4,64,768]{3,2,1,0:T(8,128)(2,1)S(1)}, u32[]{:S(2)}, u32[]{:S(2)}) %all-to-all-start.5) | async-done | bytes 1572896 | tf_op jit(solution)/shard_map/all_to_all | solution.py:120
  165.0 7.9 %collective-permute-start.20 = (bf16[400,768]{1,0:T(8,128)(2,1)}, bf16[400,768]{1,0:T(8,128)(2,1)S(1)}, u32[]{:S(2)}, u32[]{:S(2)}) collective-permute-start(bf16[400,768]{1,0:T(8,128)(2,1)} %convolution_convert_fusion), channel_id=1, source_target_pairs={{0,16},{1,17},{2,18},{3,19},{4,20},{5,21},{6,22},{7,23},{8,24},{9,... | collective-permute-start | bytes 1843208 | tf_op jit(solution)/shard_map/ppermute | solution.py:73
  174.6 6.3 %shard_map.94 = (bf16[256,1536]{1,0:T(8,128)(2,1)}, bf16[256,1536]{1,0:T(8,128)(2,1)}, bf16[256,1536]{1,0:T(8,128)(2,1)}, f32[256,1536]{1,0:T(8,128)}) custom-call(bf16[4,4,64,768]{3,2,1,0:T(8,128)(2,1)} %copy-done, bf16[1536,768]{1,0:T(8,128)(2,1)} %constant_dynamic-update-slice_fusion.2.w_ref), custom_call_target="tpu_custom_call" | custom-call | flops 2415919104 | bytes 7864320 | tf_op jit(solution)/shard_map/pallas_call | solution.py:93
  190.5 10.8 %collective-permute-done.16 = bf16[256,1536]{1,0:T(8,128)(2,1)S(1)} collective-permute-done((bf16[256,1536]{1,0:T(8,128)(2,1)}, bf16[256,1536]{1,0:T(8,128)(2,1)S(1)}, u32[]{:S(2)}, u32[]{:S(2)}) %collective-permute-start.16) | collective-permute-done | bytes 786464 | tf_op jit(solution)/shard_map/ppermute | solution.py:73
  201.3 17.7 %collective-permute-done.17 = bf16[256,1536]{1,0:T(8,128)(2,1)S(1)} collective-permute-done((bf16[256,1536]{1,0:T(8,128)(2,1)}, bf16[256,1536]{1,0:T(8,128)(2,1)S(1)}, u32[]{:S(2)}, u32[]{:S(2)}) %collective-permute-start.17) | collective-permute-done | bytes 786464 | tf_op jit(solution)/shard_map/ppermute | solution.py:73
  219.6 4.0 %collective-permute-start.22 = (bf16[64,1536]{1,0:T(8,128)(2,1)S(1)}, bf16[64,1536]{1,0:T(8,128)(2,1)S(1)}, u32[]{:S(2)}, u32[]{:S(2)}) collective-permute-start(bf16[64,1536]{1,0:T(8,128)(2,1)S(1)} %get-tuple-element.71), channel_id=1, source_target_pairs={{0,8},{1,9},{2,10},{3,11},{4,12},{5,13},{6,14},{7,15},{8,0},{9,1},... | collective-permute-start | bytes 589832 | tf_op jit(solution)/shard_map/ppermute | solution.py:73
  225.4 3.3 %convert_add_fusion = f32[768,768]{1,0:T(8,128)} fusion(bf16[384,768]{1,0:T(8,128)(2,1)} %add_convert_fusion.2, bf16[384,768]{1,0:T(8,128)(2,1)} %add_convert_fusion.3, bf16[384,768]{1,0:T(8,128)(2,1)} %collective-permute-done.28, bf16[384,768]{1,0:T(8,128)(2,1)} %collective-permute-done.27), kind=kLoop, calls=%fused_computation.1 | loop fusion | flops 5308416 | bytes 4718592 | tf_op jit(solution)/shard_map/add | solution.py:198
  229.3 9.5 %collective-permute-done.22 = bf16[64,1536]{1,0:T(8,128)(2,1)S(1)} collective-permute-done((bf16[64,1536]{1,0:T(8,128)(2,1)S(1)}, bf16[64,1536]{1,0:T(8,128)(2,1)S(1)}, u32[]{:S(2)}, u32[]{:S(2)}) %collective-permute-start.22) | collective-permute-done | bytes 196640 | tf_op jit(solution)/shard_map/ppermute | solution.py:73
  (208 shorter events, 103.4 us)
Async XLA Ops:
  12.5 31.6 %collective-permute-start.4 = (bf16[768,768]{1,0:T(8,128)(2,1)}, bf16[768,768]{1,0:T(8,128)(2,1)}, u32[]{:S(2)}, u32[]{:S(2)}) collective-permute-start(bf16[768,768]{1,0:T(8,128)(2,1)} %param.9), channel_id=1, source_target_pairs={{0,16},{1,17},{2,18},{3,19},{4,20},{5,21},{6,22},{7,23},{8,24},{9,... | collective-permute-start | bytes 3538952 | tf_op jit(solution)/shard_map/ppermute | solution.py:73
  12.6 31.5 %collective-permute-start.5 = (bf16[768,768]{1,0:T(8,128)(2,1)}, bf16[768,768]{1,0:T(8,128)(2,1)}, u32[]{:S(2)}, u32[]{:S(2)}) collective-permute-start(bf16[768,768]{1,0:T(8,128)(2,1)} %param.11), channel_id=1, source_target_pairs={{0,16},{1,17},{2,18},{3,19},{4,20},{5,21},{6,22},{7,23},{8,24},{9,... | collective-permute-start | bytes 3538952 | tf_op jit(solution)/shard_map/ppermute | solution.py:73
  15.5 17.2 %collective-permute-start.2 = (bf16[64,1536]{1,0:T(8,128)(2,1)S(1)}, bf16[64,1536]{1,0:T(8,128)(2,1)S(1)}, u32[]{:S(2)}, u32[]{:S(2)}) collective-permute-start(bf16[64,1536]{1,0:T(8,128)(2,1)S(1)} %pad_maximum_fusion.15), channel_id=1, source_target_pairs={{0,8},{1,9},{2,10},{3,11},{4,12},{5,13},{6,14},{7,15},{8,0},{9,1},... | collective-permute-start | bytes 589832 | tf_op jit(solution)/shard_map/ppermute | solution.py:73
  20.6 18.6 %collective-permute-start.1 = (bf16[64,1536]{1,0:T(8,128)(2,1)S(1)}, bf16[64,1536]{1,0:T(8,128)(2,1)S(1)}, u32[]{:S(2)}, u32[]{:S(2)}) collective-permute-start(bf16[64,1536]{1,0:T(8,128)(2,1)S(1)} %pad_maximum_fusion.15), channel_id=1, source_target_pairs={{0,12},{1,13},{2,14},{3,15},{4,0},{5,1},{6,2},{7,3},{8,4},{9,5},{1... | collective-permute-start | bytes 589832 | tf_op jit(solution)/shard_map/ppermute | solution.py:73
  24.0 19.8 %all-to-all-start = ((bf16[4,64,1536]{2,1,0:T(8,128)(2,1)}), bf16[4,64,1536]{2,1,0:T(8,128)(2,1)S(1)}, u32[]{:S(2)}, u32[]{:S(2)}) async-start(bf16[4,64,1536]{2,1,0:T(8,128)(2,1)} %broadcast_in_dim.11), calls=%async_computation | async-start | bytes 1572864 | tf_op jit(solution)/shard_map/all_to_all | solution.py:141
  40.0 19.2 %collective-permute-start.8 = (bf16[256,1536]{1,0:T(8,128)(2,1)S(1)}, bf16[256,1536]{1,0:T(8,128)(2,1)S(1)}, u32[]{:S(2)}, u32[]{:S(2)}) collective-permute-start(bf16[256,1536]{1,0:T(8,128)(2,1)S(1)} %pad_maximum_fusion.4), channel_id=1, source_target_pairs={{0,3},{1,0},{2,1},{3,2},{4,7},{5,4},{6,5},{7,6},{8,11},{9,8},{10,9... | collective-permute-start | bytes 2359304 | tf_op jit(solution)/shard_map/ppermute | solution.py:73
  42.8 19.6 %collective-permute-start.9 = (bf16[256,1536]{1,0:T(8,128)(2,1)S(1)}, bf16[256,1536]{1,0:T(8,128)(2,1)}, u32[]{:S(2)}, u32[]{:S(2)}) collective-permute-start(bf16[256,1536]{1,0:T(8,128)(2,1)S(1)} %pad_maximum_fusion.4), channel_id=1, source_target_pairs={{0,1},{1,2},{2,3},{3,0},{4,5},{5,6},{6,7},{7,4},{8,9},{9,10},{10,1... | collective-permute-start | bytes 2359304 | tf_op jit(solution)/shard_map/ppermute | solution.py:73
  44.1 50.5 %collective-permute-start.6 = (bf16[4,64,1536]{2,1,0:T(8,128)(2,1)S(1)}, bf16[4,64,1536]{2,1,0:T(8,128)(2,1)}, u32[]{:S(2)}, u32[]{:S(2)}) collective-permute-start(bf16[4,64,1536]{2,1,0:T(8,128)(2,1)S(1)} %fusion.14), channel_id=1, source_target_pairs={{0,12},{1,13},{2,14},{3,15},{4,0},{5,1},{6,2},{7,3},{8,4},{9,5},{1... | collective-permute-start | bytes 2359304 | tf_op jit(solution)/shard_map/ppermute | solution.py:73
  47.4 47.1 %collective-permute-start.7 = (bf16[4,64,1536]{2,1,0:T(8,128)(2,1)S(1)}, bf16[4,64,1536]{2,1,0:T(8,128)(2,1)}, u32[]{:S(2)}, u32[]{:S(2)}) collective-permute-start(bf16[4,64,1536]{2,1,0:T(8,128)(2,1)S(1)} %fusion.14), channel_id=1, source_target_pairs={{0,4},{1,5},{2,6},{3,7},{4,8},{5,9},{6,10},{7,11},{8,12},{9,13},{1... | collective-permute-start | bytes 2359304 | tf_op jit(solution)/shard_map/ppermute | solution.py:73
  69.6 18.0 %all-to-all-start.1 = ((bf16[4,3,64,768]{3,2,1,0:T(8,128)(2,1)}), bf16[4,3,64,768]{3,2,1,0:T(8,128)(2,1)S(1)}, u32[]{:S(2)}, u32[]{:S(2)}) async-start(bf16[4,3,64,768]{3,2,1,0:T(8,128)(2,1)} %pad_maximum_fusion.3), calls=%async_computation.1 | async-start | bytes 2359296 | tf_op jit(solution)/shard_map/all_to_all | solution.py:120
  95.6 16.8 %collective-permute-start.13 = (bf16[2,64,1536]{2,1,0:T(8,128)(2,1)S(1)}, bf16[2,64,1536]{2,1,0:T(8,128)(2,1)}, u32[]{:S(2)}, u32[]{:S(2)}) collective-permute-start(bf16[2,64,1536]{2,1,0:T(8,128)(2,1)S(1)} %slice.158), channel_id=1, source_target_pairs={{0,4},{1,5},{2,6},{3,7},{4,8},{5,9},{6,10},{7,11},{8,12},{9,13},{1... | collective-permute-start | bytes 1179656 | tf_op jit(solution)/shard_map/ppermute | solution.py:73
  102.1 20.1 %all-to-all-start.3 = ((bf16[4,4,64,768]{3,2,1,0:T(8,128)(2,1)}), bf16[4,4,64,768]{3,2,1,0:T(8,128)(2,1)S(1)}, u32[]{:S(2)}, u32[]{:S(2)}) async-start(bf16[4,4,64,768]{3,2,1,0:T(8,128)(2,1)} %broadcast_in_dim.13), calls=%async_computation.3 | async-start | bytes 3145728 | tf_op jit(solution)/shard_map/all_to_all | solution.py:120
  123.3 18.2 %all-to-all-start.4 = ((bf16[4,4,64,768]{3,2,1,0:T(8,128)(2,1)}), bf16[4,4,64,768]{3,2,1,0:T(8,128)(2,1)S(1)}, u32[]{:S(2)}, u32[]{:S(2)}) async-start(bf16[4,4,64,768]{3,2,1,0:T(8,128)(2,1)} %pad_maximum_fusion), calls=%async_computation.4 | async-start | bytes 3145728 | tf_op jit(solution)/shard_map/all_to_all | solution.py:120
  132.8 16.8 %collective-permute-start.14 = (bf16[384,768]{1,0:T(8,128)(2,1)}, bf16[384,768]{1,0:T(8,128)(2,1)}, u32[]{:S(2)}, u32[]{:S(2)}) collective-permute-start(bf16[384,768]{1,0:T(8,128)(2,1)} %convolution_convert_fusion.3), channel_id=1, source_target_pairs={{0,16},{1,17},{2,18},{3,19},{4,20},{5,21},{6,22},{7,23},{8,24},{9,... | collective-permute-start | bytes 1769480 | tf_op jit(solution)/shard_map/ppermute | solution.py:73
  143.6 17.8 %all-to-all-start.5 = ((bf16[4,4,64,768]{3,2,1,0:T(8,128)(2,1)}), bf16[4,4,64,768]{3,2,1,0:T(8,128)(2,1)S(1)}, u32[]{:S(2)}, u32[]{:S(2)}) async-start(bf16[4,4,64,768]{3,2,1,0:T(8,128)(2,1)} %broadcast_in_dim.14), calls=%async_computation.5 | async-start | bytes 3145728 | tf_op jit(solution)/shard_map/all_to_all | solution.py:120
  152.4 30.0 %collective-permute-start.27 = (bf16[384,768]{1,0:T(8,128)(2,1)}, bf16[384,768]{1,0:T(8,128)(2,1)}, u32[]{:S(2)}, u32[]{:S(2)}) collective-permute-start(bf16[384,768]{1,0:T(8,128)(2,1)} %add_convert_fusion.3), channel_id=1, source_target_pairs={{0,128},{1,129},{2,130},{3,131},{4,132},{5,133},{6,134},{7,135},{8... | collective-permute-start | bytes 1769480 | tf_op jit(solution)/shard_map/ppermute | solution.py:73
  155.1 28.4 %collective-permute-start.28 = (bf16[384,768]{1,0:T(8,128)(2,1)}, bf16[384,768]{1,0:T(8,128)(2,1)}, u32[]{:S(2)}, u32[]{:S(2)}) collective-permute-start(bf16[384,768]{1,0:T(8,128)(2,1)} %add_convert_fusion.2), channel_id=1, source_target_pairs={{0,128},{1,129},{2,130},{3,131},{4,132},{5,133},{6,134},{7,135},{8... | collective-permute-start | bytes 1769480 | tf_op jit(solution)/shard_map/ppermute | solution.py:73
  165.0 20.2 %collective-permute-start.20 = (bf16[400,768]{1,0:T(8,128)(2,1)}, bf16[400,768]{1,0:T(8,128)(2,1)S(1)}, u32[]{:S(2)}, u32[]{:S(2)}) collective-permute-start(bf16[400,768]{1,0:T(8,128)(2,1)} %convolution_convert_fusion), channel_id=1, source_target_pairs={{0,16},{1,17},{2,18},{3,19},{4,20},{5,21},{6,22},{7,23},{8,24},{9,... | collective-permute-start | bytes 1843208 | tf_op jit(solution)/shard_map/ppermute | solution.py:73
  180.9 20.4 %collective-permute-start.16 = (bf16[256,1536]{1,0:T(8,128)(2,1)}, bf16[256,1536]{1,0:T(8,128)(2,1)S(1)}, u32[]{:S(2)}, u32[]{:S(2)}) collective-permute-start(bf16[256,1536]{1,0:T(8,128)(2,1)} %get-tuple-element.54), channel_id=1, source_target_pairs={{0,2},{1,3},{2,0},{3,1},{4,6},{5,7},{6,4},{7,5},{8,10},{9,11},{10,... | collective-permute-start | bytes 2359304 | tf_op jit(solution)/shard_map/ppermute | solution.py:73
  182.4 36.5 %collective-permute-start.17 = (bf16[256,1536]{1,0:T(8,128)(2,1)}, bf16[256,1536]{1,0:T(8,128)(2,1)S(1)}, u32[]{:S(2)}, u32[]{:S(2)}) collective-permute-start(bf16[256,1536]{1,0:T(8,128)(2,1)} %get-tuple-element.55), channel_id=1, source_target_pairs={{0,1},{1,2},{2,3},{3,0},{4,5},{5,6},{6,7},{7,4},{8,9},{9,10},{10,1... | collective-permute-start | bytes 2359304 | tf_op jit(solution)/shard_map/ppermute | solution.py:73
  183.6 35.4 %collective-permute-start.18 = (bf16[256,1536]{1,0:T(8,128)(2,1)}, bf16[256,1536]{1,0:T(8,128)(2,1)S(1)}, u32[]{:S(2)}, u32[]{:S(2)}) collective-permute-start(bf16[256,1536]{1,0:T(8,128)(2,1)} %get-tuple-element.56), channel_id=1, source_target_pairs={{0,3},{1,0},{2,1},{3,2},{4,7},{5,4},{6,5},{7,6},{8,11},{9,8},{10,9... | collective-permute-start | bytes 2359304 | tf_op jit(solution)/shard_map/ppermute | solution.py:73
  187.1 52.8 %collective-permute-start.24 = (bf16[384,768]{1,0:T(8,128)(2,1)S(1)}, bf16[384,768]{1,0:T(8,128)(2,1)S(1)}, u32[]{:S(2)}, u32[]{:S(2)}) collective-permute-start(bf16[384,768]{1,0:T(8,128)(2,1)S(1)} %add_convert_fusion.1), channel_id=1, source_target_pairs={{0,128},{1,129},{2,130},{3,131},{4,132},{5,133},{6,134},{7,135},{8... | collective-permute-start | bytes 1769480 | tf_op jit(solution)/shard_map/ppermute | solution.py:73
  188.9 51.1 %collective-permute-start.25 = (bf16[400,768]{1,0:T(8,128)(2,1)S(1)}, bf16[400,768]{1,0:T(8,128)(2,1)S(1)}, u32[]{:S(2)}, u32[]{:S(2)}) collective-permute-start(bf16[400,768]{1,0:T(8,128)(2,1)S(1)} %pad_maximum_fusion.9), channel_id=1, source_target_pairs={{0,128},{1,129},{2,130},{3,131},{4,132},{5,133},{6,134},{7,135},{8... | collective-permute-start | bytes 1843208 | tf_op jit(solution)/shard_map/ppermute | solution.py:73
  219.6 19.1 %collective-permute-start.22 = (bf16[64,1536]{1,0:T(8,128)(2,1)S(1)}, bf16[64,1536]{1,0:T(8,128)(2,1)S(1)}, u32[]{:S(2)}, u32[]{:S(2)}) collective-permute-start(bf16[64,1536]{1,0:T(8,128)(2,1)S(1)} %get-tuple-element.71), channel_id=1, source_target_pairs={{0,8},{1,9},{2,10},{3,11},{4,12},{5,13},{6,14},{7,15},{8,0},{9,1},... | collective-permute-start | bytes 589832 | tf_op jit(solution)/shard_map/ppermute | solution.py:73
  (56 other events, 410.5 us)
